TPU v7x, 32 devices: a whole 2x2x4 slice. The times are simulated.
32 devices in a mesh: tm: 4 (over z), lat: 4 (over y, core), lon: 2 (over x).
Axes of the slice: x: 2, y: 2, z: 4, core: 2. Of those that a mesh axis runs over, the one named last changes fastest.
Arguments:
- depth_class: int32 [544, 768], P('lat', 'lon'), may hold values from 0 to 31
- ocean_mask: int32 [544, 768], P('lat', 'lon'), may hold values 0 or 1
- depth_levels: float32 [32], replicated, may hold values from 0.1 to 1
- drag: float32 [544, 768], P('lat', 'lon'), may hold values from 0.0005 to 0.02
- tide_force: float32 [2, 544, 768], P(None, 'lat', 'lon'), may hold values from -6 to 6
- forward_flow: float32 [4, 544, 768], P(None, 'lat', 'lon'), may hold values from -6 to 6
- guess: float32 [4, 3, 544, 768], P('tm', None, 'lat', 'lon'), may hold values from -4 to 4
Outputs:
- final_state: float32 [4, 3, 544, 768], P('tm', None, 'lat', 'lon')
- drag_gradient: float32 [544, 768], P('lat', 'lon')
Inputs may be any that keep to these rules, and one draw needn't show every extreme that they name: `depth_class`: index into depth_levels.
All inputs are finite; a program needn't handle non-finite values. No bound on the sum of `ocean_mask` on one device may be relied on, other than what follows from the above.
Results may differ from a plain program's by a relative error of at most 0.00002.
Values sent between devices are 32-bit elements; how exact they have to be, the bound alone decides.
A program may use at most 64 MiB of HBM per device.

v0:
```python
import math

import jax
import jax.numpy as jnp
from jax import lax
from jax.sharding import PartitionSpec as P

STEPS = 16
SWEEPS = 2
DCLASS = 32


gravity_coef = 0.7
flux_coef = 0.6


def padded_2(block, sides, width):
    for axis, dim in sides:
        count = lax.axis_size(axis)
        forward = [(i, i + 1) for i in range(count - 1)]
        forward.append((count - 1, 0))
        backward = [(target, source) for source, target in forward]
        low = lax.ppermute(
            lax.slice_in_dim(block, block.shape[dim] - width, None, axis=dim), axis, forward
        )
        high = lax.ppermute(lax.slice_in_dim(block, 0, width, axis=dim), axis, backward)
        block = jnp.concatenate([low, block, high], axis=dim)
    return block


def shifted(value, axis, steps):
    count = lax.axis_size(axis)
    pairs = [(source, (source + steps) % count) for source in range(count)]
    return lax.ppermute(value, axis, pairs)


def shifted_2(block, axis, distance):
    devices = range(lax.axis_size(axis))
    route = [(i - distance, i) for i in devices if i - distance in devices]
    return lax.ppermute(block, axis, route)


def trim(field, margin):
    rows = field.shape[-2]
    cols = field.shape[-1]
    return field[..., margin : rows - margin, margin : cols - margin]


def advance(padded, margin, faces, wide, cosine, sine):
    offset = wide - margin
    depth_u, depth_v, mask_u, mask_v, damp_u, damp_v, mask_c, force_c, force_s = [
        trim(f, offset) for f in faces
    ]
    elev, zonal, merid = (padded[0], padded[1], padded[2])
    zonal_new = mask_u[1:-1, 1:] * (
        damp_u[1:-1, 1:] * zonal[1:-1, 1:] - gravity_coef * (elev[1:-1, 1:] - elev[1:-1, :-1])
    )
    merid_new = mask_v[1:, 1:-1] * (
        damp_v[1:, 1:-1] * merid[1:, 1:-1] - gravity_coef * (elev[1:, 1:-1] - elev[:-1, 1:-1])
    )
    flux_u = depth_u[1:-1, 1:] * zonal_new
    flux_v = depth_v[1:, 1:-1] * merid_new
    spread = flux_u[:, 1:] - flux_u[:, :-1] + (flux_v[1:, :] - flux_v[:-1, :])
    source = force_c[1:-1, 1:-1] * cosine + force_s[1:-1, 1:-1] * sine
    elev_new = mask_c[1:-1, 1:-1] * (elev[1:-1, 1:-1] - flux_coef * spread + source)
    state = jnp.stack([elev_new, zonal_new[:, :-1], merid_new[:-1, :]])
    return (state, zonal_new, merid_new)


def shards(depth_class, ocean_mask, depth_levels, drag, tide_force, forward_flow, guess):
    rows, cols = ocean_mask.shape
    tm_size = lax.axis_size("tm")
    total_rows = rows * lax.axis_size("lat")
    wide = 4

    def widen(state):
        return padded_2(state, (("lat", 1), ("lon", 2)), 4)

    classes = jnp.arange(DCLASS, dtype=jnp.int32)
    depth = jnp.sum(
        jnp.where(
            depth_class[None] == classes[:, None, None],
            depth_levels[:, None, None],
            jnp.float32(0.0),
        ),
        axis=0,
    )
    row_index = lax.axis_index("lat") * rows + jnp.arange(rows, dtype=jnp.int32)
    polar = (row_index == 0) | (row_index == total_rows - 1)
    mask = jnp.where(polar[:, None], 0, ocean_mask).astype(jnp.float32)
    stacked = jnp.stack([depth, mask, drag, tide_force[0], tide_force[1]])
    padded = padded_2(stacked, (("lat", 1), ("lon", 2)), wide + 1)
    center = padded[:, 1:-1, 1:-1]
    west_side = padded[:, 1:-1, :-2]
    south_side = padded[:, :-2, 1:-1]
    depth_u = 0.5 * (center[0] + west_side[0])
    mask_u = center[1] * west_side[1]
    damp_u = 1.0 - (center[2] + west_side[2]) / (center[0] + west_side[0])
    depth_v = 0.5 * (center[0] + south_side[0])
    mask_v = center[1] * south_side[1]
    damp_v = 1.0 - (center[2] + south_side[2]) / (center[0] + south_side[0])
    faces = (depth_u, depth_v, mask_u, mask_v, damp_u, damp_v, center[1], center[3], center[4])
    weight = mask / depth
    gain = jnp.stack(
        [
            mask,
            trim(mask_u, wide) * trim(damp_u, wide) ** STEPS,
            trim(mask_v, wide) * trim(damp_v, wide) ** STEPS,
        ]
    )
    cycle = jnp.float32(tm_size * STEPS)
    slice_index = lax.axis_index("tm")
    bound = guess[0]
    total = jnp.zeros((rows, cols), jnp.float32)
    for sweep in range(SWEEPS):
        want = sweep == SWEEPS - 1

        def block(number, carry):
            state, term = carry
            extended = widen(state)
            for sub in range(wide):
                count = slice_index * STEPS + number * wide + sub + 1
                angle = jnp.float32(2.0 * math.pi) * count.astype(jnp.float32) / cycle
                cosine, sine = (jnp.cos(angle), jnp.sin(angle))
                margin = wide - sub
                extended, zonal_new, merid_new = advance(
                    extended, margin, faces, wide, cosine, sine
                )
                if want:
                    lead = margin - 1
                    flow_u = forward_flow[0] * cosine + forward_flow[1] * sine
                    flow_v = forward_flow[2] * cosine + forward_flow[3] * sine
                    u_mid = 0.5 * (
                        zonal_new[lead : lead + rows, lead : lead + cols]
                        + zonal_new[lead : lead + rows, lead + 1 : lead + 1 + cols]
                    )
                    v_mid = 0.5 * (
                        merid_new[lead : lead + rows, lead : lead + cols]
                        + merid_new[lead + 1 : lead + 1 + rows, lead : lead + cols]
                    )
                    term = term + weight * (flow_u * u_mid + flow_v * v_mid)
            return (extended, term)

        zeros = jnp.zeros((rows, cols), jnp.float32)
        end, term = lax.fori_loop(0, STEPS // wide, block, (bound, zeros))
        if want:
            total = term
        arrived = shifted(end, "tm", 1)
        jump = arrived - bound

        def relay(turn, change_now):
            return jump + gain * shifted_2(change_now, "tm", 1)

        change = lax.fori_loop(0, tm_size - 1, relay, jump)
        bound = bound + change
    summed = lax.psum(total, "tm")
    drag_gradient = summed / jnp.float32(tm_size * STEPS)
    return (bound[None], drag_gradient)


def solution(mesh):
    return jax.shard_map(
        shards,
        mesh=mesh,
        in_specs=(
            P("lat", "lon"),
            P("lat", "lon"),
            P(),
            P("lat", "lon"),
            P(None, "lat", "lon"),
            P(None, "lat", "lon"),
            P("tm", None, "lat", "lon"),
        ),
        out_specs=(P("tm", None, "lat", "lon"), P("lat", "lon")),
        check_vma=False,
    )
```

profile of v0, /device:TPU:0, one launch (start us, length us, event | category | flops | bytes accessed | tf_op | source)
XLA Modules:
  0.0 403.9 jit_solution(13043040371950531608)
XLA Ops:
  8.3 1.8 select_reduce_fusion
  11.5 2.0 collective-permute-start.11
  13.5 1.8 collective-permute-done.10
  16.8 1.8 collective-permute-start.12
  18.9 9.1 %collective-permute-done.12 = f32[5,146,5]{2,1,0:T(8,128)S(1)} collective-permute-done((f32[5,146,5]{2,1,0:T(8,128)}, f32[5,146,5]{2,1,0:T(8,128)S(1)}, u32[]{:S(2)}, u32[]{:S(2)}) %collective-permute-start.12) | collective-permute-done | bytes 14632 | tf_op jit(solution)/shard_map/ppermute | solution.py:23
  27.9 8.3 %collective-permute-done.13 = f32[5,146,5]{2,1,0:T(8,128)S(1)} collective-permute-done((f32[5,146,5]{2,1,0:T(8,128)S(1)}, f32[5,146,5]{2,1,0:T(8,128)S(1)}, u32[]{:S(2)}, u32[]{:S(2)}) %collective-permute-start.13) | collective-permute-done | bytes 14632 | tf_op jit(solution)/shard_map/ppermute | solution.py:26
  36.3 1.5 pad_maximum_fusion.10
  38.7 95.5 %while.55 = (s32[]{:T(128)}, f32[3,136,384]{2,1,0:T(8,128)S(1)}, f32[144,392]{1,0:T(8,128)S(1)}, f32[144,392]{1,0:T(8,128)S(1)}, f32[144,392]{1,0:T(8,128)S(1)},...) while((s32[]{:T(128)}, f32[3,136,384]{2,1,0:T(8,128)S(1)}, ...), condition=%wide.region_2.3_spmd, body=%wide.region_1.2_spmd.sunk | while | flops 5744496 | bytes 27339412 | solution.py:145
  38.7 1.4 collective-permute-start
  40.1 1.5 collective-permute-done
  41.6 1.7 collective-permute-done.1
  44.1 2.0 collective-permute-start.2
  46.8 6.0 %collective-permute-done.2 = f32[3,144,4]{2,1,0:T(8,128)} collective-permute-done((f32[3,144,4]{2,1,0:T(8,128)}, f32[3,144,4]{2,1,0:T(8,128)}, u32[]{:S(2)}, u32[]{:S(2)}) %collective-permute-start.2) | collective-permute-done | bytes 6944 | tf_op jit(solution)/shard_map/while/body/eval_jaxpr/ppermute | solution.py:26
  52.8 3.2 collective-permute-done.3
  65.2 1.8 collective-permute-done.1
  67.8 1.7 collective-permute-start.2
  70.4 6.0 %collective-permute-done.2 = f32[3,144,4]{2,1,0:T(8,128)} collective-permute-done((f32[3,144,4]{2,1,0:T(8,128)}, f32[3,144,4]{2,1,0:T(8,128)}, u32[]{:S(2)}, u32[]{:S(2)}) %collective-permute-start.2) | collective-permute-done | bytes 6944 | tf_op jit(solution)/shard_map/while/body/eval_jaxpr/ppermute | solution.py:26
  76.5 3.2 collective-permute-done.3
  88.8 1.8 collective-permute-done.1
  91.4 1.7 collective-permute-start.2
  94.0 6.0 %collective-permute-done.2 = f32[3,144,4]{2,1,0:T(8,128)} collective-permute-done((f32[3,144,4]{2,1,0:T(8,128)}, f32[3,144,4]{2,1,0:T(8,128)}, u32[]{:S(2)}, u32[]{:S(2)}) %collective-permute-start.2) | collective-permute-done | bytes 6944 | tf_op jit(solution)/shard_map/while/body/eval_jaxpr/ppermute | solution.py:26
  100.1 2.9 collective-permute-done.3
  103.0 1.4 pad_maximum_fusion.29
  112.1 1.8 collective-permute-done.1
  114.7 1.7 collective-permute-start.2
  117.3 6.0 %collective-permute-done.2 = f32[3,144,4]{2,1,0:T(8,128)} collective-permute-done((f32[3,144,4]{2,1,0:T(8,128)}, f32[3,144,4]{2,1,0:T(8,128)}, u32[]{:S(2)}, u32[]{:S(2)}) %collective-permute-start.2) | collective-permute-done | bytes 6944 | tf_op jit(solution)/shard_map/while/body/eval_jaxpr/ppermute | solution.py:26
  123.4 3.2 collective-permute-done.3
  134.1 2.1 collective-permute-start.14
  137.7 1.8 pad_maximum_fusion.11
  139.5 11.7 %collective-permute-done.14 = f32[3,136,384]{2,1,0:T(8,128)} collective-permute-done((f32[3,136,384]{2,1,0:T(8,128)S(1)}, f32[3,136,384]{2,1,0:T(8,128)}, u32[]{:S(2)}, u32[]{:S(2)}) %collective-permute-start.14) | collective-permute-done | bytes 626720 | tf_op jit(solution)/shard_map/ppermute | solution.py:34
  153.5 49.4 %while.56 = (s32[]{:T(128)}, f32[3,136,384]{2,1,0:T(8,128)}, f32[3,136,384]{2,1,0:T(8,128)S(1)}, f32[3,136,384]{2,1,0:T(8,128)}, s32[]{:T(128)}) while((s32[]{:T(128)}, f32[3,136,384]{2,1,0:T(8,128)}, f32[3,136,384]{2,1,0:T(8,128)S(1)}, f32[3,136,384]{2,1,0:T(8,128)}, s32[]{:T(128)}) %tuple.216), condition=%wide.region_4.5_spmd, body=%wide.region_3.4_spmd.sunk | while | flops 313346 | bytes 5013605 | solution.py:154
  153.5 2.5 collective-permute-start.4
  156.0 10.9 %collective-permute-done.4 = f32[3,136,384]{2,1,0:T(8,128)} collective-permute-done((f32[3,136,384]{2,1,0:T(8,128)}, f32[3,136,384]{2,1,0:T(8,128)}, u32[]{:S(2)}, u32[]{:S(2)}) %collective-permute-start.4) | collective-permute-done | bytes 626720 | tf_op jit(solution)/shard_map/while/body/eval_jaxpr/ppermute | solution.py:40
  166.8 2.2 multiply_add_fusion.4
  169.1 5.2 %collective-permute-start.4 = (f32[3,136,384]{2,1,0:T(8,128)}, f32[3,136,384]{2,1,0:T(8,128)}, u32[]{:S(2)}, u32[]{:S(2)}) collective-permute-start(f32[3,136,384]{2,1,0:T(8,128)} %get-tuple-element.1340), channel_id=1, source_target_pairs={{0,8},{8,16},{16,24},{1,9},{9,17},{17,25},{2,10},{10,18},{18,26},{... | collective-permute-start | bytes 1880072 | tf_op jit(solution)/shard_map/while/body/eval_jaxpr/ppermute | solution.py:40
  174.3 9.9 %collective-permute-done.4 = f32[3,136,384]{2,1,0:T(8,128)} collective-permute-done((f32[3,136,384]{2,1,0:T(8,128)}, f32[3,136,384]{2,1,0:T(8,128)}, u32[]{:S(2)}, u32[]{:S(2)}) %collective-permute-start.4) | collective-permute-done | bytes 626720 | tf_op jit(solution)/shard_map/while/body/eval_jaxpr/ppermute | solution.py:40
  184.2 2.2 multiply_add_fusion.4
  186.4 5.2 %collective-permute-start.4 = (f32[3,136,384]{2,1,0:T(8,128)}, f32[3,136,384]{2,1,0:T(8,128)}, u32[]{:S(2)}, u32[]{:S(2)}) collective-permute-start(f32[3,136,384]{2,1,0:T(8,128)} %get-tuple-element.1340), channel_id=1, source_target_pairs={{0,8},{8,16},{16,24},{1,9},{9,17},{17,25},{2,10},{10,18},{18,26},{... | collective-permute-start | bytes 1880072 | tf_op jit(solution)/shard_map/while/body/eval_jaxpr/ppermute | solution.py:40
  191.7 9.0 %collective-permute-done.4 = f32[3,136,384]{2,1,0:T(8,128)} collective-permute-done((f32[3,136,384]{2,1,0:T(8,128)}, f32[3,136,384]{2,1,0:T(8,128)}, u32[]{:S(2)}, u32[]{:S(2)}) %collective-permute-start.4) | collective-permute-done | bytes 626720 | tf_op jit(solution)/shard_map/while/body/eval_jaxpr/ppermute | solution.py:40
  200.7 2.2 multiply_add_fusion.4
  205.1 103.2 %while.58 = (s32[]{:T(128)}, f32[3,136,384]{2,1,0:T(8,128)S(1)}, f32[136,384]{1,0:T(8,128)}, f32[144,392]{1,0:T(8,128)S(1)}, f32[144,392]{1,0:T(8,128)S(1)}, /*i...) while((s32[]{:T(128)}, f32[3,136,384]{2,1,0:T(8,128)S(1)}, ...), condition=%wide.region_6.7_spmd.clone, body=%wide.region_5.6_spmd.clone.sunk | while | flops 8930161 | bytes 37157688 | solution.py:145
  206.7 1.8 collective-permute-done.7
  211.9 5.8 %collective-permute-done.8 = f32[3,144,4]{2,1,0:T(8,128)} collective-permute-done((f32[3,144,4]{2,1,0:T(8,128)}, f32[3,144,4]{2,1,0:T(8,128)}, u32[]{:S(2)}, u32[]{:S(2)}) %collective-permute-start.8) | collective-permute-done | bytes 6944 | tf_op jit(solution)/shard_map/while/body/eval_jaxpr/ppermute | solution.py:26
  217.8 2.4 collective-permute-done.9
  231.0 1.5 collective-permute-done.6
  232.4 1.7 collective-permute-done.7
  237.7 6.0 %collective-permute-done.8 = f32[3,144,4]{2,1,0:T(8,128)} collective-permute-done((f32[3,144,4]{2,1,0:T(8,128)}, f32[3,144,4]{2,1,0:T(8,128)}, u32[]{:S(2)}, u32[]{:S(2)}) %collective-permute-start.8) | collective-permute-done | bytes 6944 | tf_op jit(solution)/shard_map/while/body/eval_jaxpr/ppermute | solution.py:26
  243.7 3.2 collective-permute-done.9
  258.3 1.8 collective-permute-done.7
  263.6 6.0 %collective-permute-done.8 = f32[3,144,4]{2,1,0:T(8,128)} collective-permute-done((f32[3,144,4]{2,1,0:T(8,128)}, f32[3,144,4]{2,1,0:T(8,128)}, u32[]{:S(2)}, u32[]{:S(2)}) %collective-permute-start.8) | collective-permute-done | bytes 6944 | tf_op jit(solution)/shard_map/while/body/eval_jaxpr/ppermute | solution.py:26
  269.6 2.9 collective-permute-done.9
  284.0 1.8 collective-permute-done.7
  289.2 6.0 %collective-permute-done.8 = f32[3,144,4]{2,1,0:T(8,128)} collective-permute-done((f32[3,144,4]{2,1,0:T(8,128)}, f32[3,144,4]{2,1,0:T(8,128)}, u32[]{:S(2)}, u32[]{:S(2)}) %collective-permute-start.8) | collective-permute-done | bytes 6944 | tf_op jit(solution)/shard_map/while/body/eval_jaxpr/ppermute | solution.py:26
  295.3 3.1 collective-permute-done.9
  308.3 2.5 collective-permute-start.15
  310.8 37.4 %all-reduce.2.cloned.1.call-done = f32[136,384]{1,0:T(8,128)} async-done(((f32[136,384]{1,0:T(8,128)}), f32[136,384]{1,0:T(8,128)}) %all-reduce.2.cloned.1.call-update) | async-done | bytes 208912 | tf_op jit(solution)/shard_map/psum | solution.py:156
  348.2 1.6 broadcast_multiply_fusion
  351.2 44.9 %while.57 = (s32[]{:T(128)}, f32[3,136,384]{2,1,0:T(8,128)S(1)}, f32[3,136,384]{2,1,0:T(8,128)S(1)}, f32[3,136,384]{2,1,0:T(8,128)S(1)}, s32[]{:T(128)}) while((s32[]{:T(128)}, f32[3,136,384]{2,1,0:T(8,128)S(1)}, f32[3,136,384]{2,1,0:T(8,128)S(1)}, f32[3,136,384]{2,1,0:T(8,128)S(1)}, s32[]{:T(128)}) %tuple.215), condition=%wide.region_8.9_spmd, body=%wide.region_7.8_spmd.sunk | while | flops 313346 | bytes 5013605 | solution.py:154
  351.2 3.9 collective-permute-start.5
  355.1 11.5 %collective-permute-done.5 = f32[3,136,384]{2,1,0:T(8,128)S(1)} collective-permute-done((f32[3,136,384]{2,1,0:T(8,128)S(1)}, f32[3,136,384]{2,1,0:T(8,128)S(1)}, u32[]{:S(2)}, u32[]{:S(2)}) %collective-permute-start.5) | collective-permute-done | bytes 626720 | tf_op jit(solution)/shard_map/while/body/eval_jaxpr/ppermute | solution.py:40
  366.7 4.4 %collective-permute-start.5 = (f32[3,136,384]{2,1,0:T(8,128)S(1)}, f32[3,136,384]{2,1,0:T(8,128)S(1)}, u32[]{:S(2)}, u32[]{:S(2)}) collective-permute-start(f32[3,136,384]{2,1,0:T(8,128)S(1)} %get-tuple-element.1418), channel_id=1, source_target_pairs={{0,8},{8,16},{16,24},{1,9},{9,17},{17,25},{2,10},{10,18},{18,26},{... | collective-permute-start | bytes 1880072 | tf_op jit(solution)/shard_map/while/body/eval_jaxpr/ppermute | solution.py:40
  371.1 10.6 %collective-permute-done.5 = f32[3,136,384]{2,1,0:T(8,128)S(1)} collective-permute-done((f32[3,136,384]{2,1,0:T(8,128)S(1)}, f32[3,136,384]{2,1,0:T(8,128)S(1)}, u32[]{:S(2)}, u32[]{:S(2)}) %collective-permute-start.5) | collective-permute-done | bytes 626720 | tf_op jit(solution)/shard_map/while/body/eval_jaxpr/ppermute | solution.py:40
  381.9 4.4 %collective-permute-start.5 = (f32[3,136,384]{2,1,0:T(8,128)S(1)}, f32[3,136,384]{2,1,0:T(8,128)S(1)}, u32[]{:S(2)}, u32[]{:S(2)}) collective-permute-start(f32[3,136,384]{2,1,0:T(8,128)S(1)} %get-tuple-element.1418), channel_id=1, source_target_pairs={{0,8},{8,16},{16,24},{1,9},{9,17},{17,25},{2,10},{10,18},{18,26},{... | collective-permute-start | bytes 1880072 | tf_op jit(solution)/shard_map/while/body/eval_jaxpr/ppermute | solution.py:40
  386.3 9.6 %collective-permute-done.5 = f32[3,136,384]{2,1,0:T(8,128)S(1)} collective-permute-done((f32[3,136,384]{2,1,0:T(8,128)S(1)}, f32[3,136,384]{2,1,0:T(8,128)S(1)}, u32[]{:S(2)}, u32[]{:S(2)}) %collective-permute-start.5) | collective-permute-done | bytes 626720 | tf_op jit(solution)/shard_map/while/body/eval_jaxpr/ppermute | solution.py:40
  (254 shorter events, 107.4 us)
Async XLA Ops:
  7.2 8.7 %copy-start.12 = (f32[2,136,384]{2,1,0:T(8,128)S(1)}, f32[2,136,384]{2,1,0:T(8,128)}, u32[]{:S(2)}) copy-start(f32[2,136,384]{2,1,0:T(8,128)} %param.19) | copy-start | bytes 1253380
  7.2 8.7 %copy-start.13 = (f32[136,384]{1,0:T(8,128)S(1)}, f32[136,384]{1,0:T(8,128)}, u32[]{:S(2)}) copy-start(f32[136,384]{1,0:T(8,128)} %param.18) | copy-start | bytes 626692
  7.2 341.0 %all-reduce.2.cloned.1.call-start = ((), (), s32[]{:S(2)}) async-start(), calls=%async_computation | async-start | bytes 417792 | tf_op jit(solution)/shard_map/psum | solution.py:156
  8.3 27.9 %copy-start.10 = (f32[1,136,384]{2,1,0:T(8,128)}, f32[1,136,384]{2,1,0:T(8,128)S(1)}, u32[]{:S(2)}) copy-start(f32[1,136,384]{2,1,0:T(8,128)S(1)} %convert_bitcast_fusion) | copy-start | bytes 626692
  10.1 26.2 %copy-start.11 = (f32[136,384]{1,0:T(8,128)}, f32[136,384]{1,0:T(8,128)S(1)}, u32[]{:S(2)}) copy-start(f32[136,384]{1,0:T(8,128)S(1)} %select_reduce_fusion) | copy-start | bytes 626692
  10.1 8.7 %copy-start.8 = (f32[1,3,136,384]{3,2,1,0:T(8,128)S(1)}, f32[1,3,136,384]{3,2,1,0:T(8,128)}, u32[]{:S(2)}) copy-start(f32[1,3,136,384]{3,2,1,0:T(8,128)} %param.21) | copy-start | bytes 1880068
  11.0 4.4 %collective-permute-start.10 = (f32[5,5,384]{2,1,0:T(8,128)S(1)}, f32[5,5,384]{2,1,0:T(8,128)S(1)}, u32[]{:S(2)}, u32[]{:S(2)}) collective-permute-start(f32[5,5,384]{2,1,0:T(8,128)S(1)} %get-tuple-element.965), channel_id=1, source_target_pairs={{0,2},{2,4},{4,6},{6,0},{1,3},{3,5},{5,7},{7,1},{8,10},{10,12},{12... | collective-permute-start | bytes 115208 | tf_op jit(solution)/shard_map/ppermute | solution.py:23
  11.5 4.3 %collective-permute-start.11 = (f32[5,5,384]{2,1,0:T(8,128)S(1)}, f32[5,5,384]{2,1,0:T(8,128)S(1)}, u32[]{:S(2)}, u32[]{:S(2)}) collective-permute-start(f32[5,5,384]{2,1,0:T(8,128)S(1)} %get-tuple-element.966), channel_id=1, source_target_pairs={{2,0},{4,2},{6,4},{0,6},{3,1},{5,3},{7,5},{1,7},{10,8},{12,10},{14... | collective-permute-start | bytes 115208 | tf_op jit(solution)/shard_map/ppermute | solution.py:26
  15.8 0.9 copy-start.14
  16.8 11.1 %collective-permute-start.12 = (f32[5,146,5]{2,1,0:T(8,128)}, f32[5,146,5]{2,1,0:T(8,128)S(1)}, u32[]{:S(2)}, u32[]{:S(2)}) collective-permute-start(f32[5,146,5]{2,1,0:T(8,128)} %get-tuple-element.963), channel_id=1, source_target_pairs={{0,1},{1,0},{2,3},{3,2},{4,5},{5,4},{6,7},{7,6},{8,9},{9,8},{10,11... | collective-permute-start | bytes 43808 | tf_op jit(solution)/shard_map/ppermute | solution.py:23
  18.6 17.7 %collective-permute-start.13 = (f32[5,146,5]{2,1,0:T(8,128)S(1)}, f32[5,146,5]{2,1,0:T(8,128)S(1)}, u32[]{:S(2)}, u32[]{:S(2)}) collective-permute-start(f32[5,146,5]{2,1,0:T(8,128)S(1)} %get-tuple-element.964), channel_id=1, source_target_pairs={{1,0},{0,1},{3,2},{2,3},{5,4},{4,5},{7,6},{6,7},{9,8},{8,9},{11,10... | collective-permute-start | bytes 43808 | tf_op jit(solution)/shard_map/ppermute | solution.py:26
  38.7 2.9 collective-permute-start
  40.1 3.2 collective-permute-start.1
  44.1 8.7 %collective-permute-start.2 = (f32[3,144,4]{2,1,0:T(8,128)}, f32[3,144,4]{2,1,0:T(8,128)}, u32[]{:S(2)}, u32[]{:S(2)}) collective-permute-start(f32[3,144,4]{2,1,0:T(8,128)} %get-tuple-element.1212), channel_id=1, source_target_pairs={{1,0},{0,1},{3,2},{2,3},{5,4},{4,5},{7,6},{6,7},{9,8},{8,9},{11,10... | collective-permute-start | bytes 20744 | tf_op jit(solution)/shard_map/while/body/eval_jaxpr/ppermute | solution.py:26
  46.1 9.9 %collective-permute-start.3 = (f32[3,144,4]{2,1,0:T(8,128)}, f32[3,144,4]{2,1,0:T(8,128)}, u32[]{:S(2)}, u32[]{:S(2)}) collective-permute-start(f32[3,144,4]{2,1,0:T(8,128)} %get-tuple-element.1213), channel_id=1, source_target_pairs={{0,1},{1,0},{2,3},{3,2},{4,5},{5,4},{6,7},{7,6},{8,9},{9,8},{10,11... | collective-permute-start | bytes 20744 | tf_op jit(solution)/shard_map/while/body/eval_jaxpr/ppermute | solution.py:23
  63.6 1.5 collective-permute-start
  63.7 3.2 collective-permute-start.1
  67.8 8.7 %collective-permute-start.2 = (f32[3,144,4]{2,1,0:T(8,128)}, f32[3,144,4]{2,1,0:T(8,128)}, u32[]{:S(2)}, u32[]{:S(2)}) collective-permute-start(f32[3,144,4]{2,1,0:T(8,128)} %get-tuple-element.1212), channel_id=1, source_target_pairs={{1,0},{0,1},{3,2},{2,3},{5,4},{4,5},{7,6},{6,7},{9,8},{8,9},{11,10... | collective-permute-start | bytes 20744 | tf_op jit(solution)/shard_map/while/body/eval_jaxpr/ppermute | solution.py:26
  69.5 10.1 %collective-permute-start.3 = (f32[3,144,4]{2,1,0:T(8,128)}, f32[3,144,4]{2,1,0:T(8,128)}, u32[]{:S(2)}, u32[]{:S(2)}) collective-permute-start(f32[3,144,4]{2,1,0:T(8,128)} %get-tuple-element.1213), channel_id=1, source_target_pairs={{0,1},{1,0},{2,3},{3,2},{4,5},{5,4},{6,7},{7,6},{8,9},{9,8},{10,11... | collective-permute-start | bytes 20744 | tf_op jit(solution)/shard_map/while/body/eval_jaxpr/ppermute | solution.py:23
  87.2 1.5 collective-permute-start
  87.3 3.2 collective-permute-start.1
  91.4 8.7 %collective-permute-start.2 = (f32[3,144,4]{2,1,0:T(8,128)}, f32[3,144,4]{2,1,0:T(8,128)}, u32[]{:S(2)}, u32[]{:S(2)}) collective-permute-start(f32[3,144,4]{2,1,0:T(8,128)} %get-tuple-element.1212), channel_id=1, source_target_pairs={{1,0},{0,1},{3,2},{2,3},{5,4},{4,5},{7,6},{6,7},{9,8},{8,9},{11,10... | collective-permute-start | bytes 20744 | tf_op jit(solution)/shard_map/while/body/eval_jaxpr/ppermute | solution.py:26
  93.1 9.8 %collective-permute-start.3 = (f32[3,144,4]{2,1,0:T(8,128)}, f32[3,144,4]{2,1,0:T(8,128)}, u32[]{:S(2)}, u32[]{:S(2)}) collective-permute-start(f32[3,144,4]{2,1,0:T(8,128)} %get-tuple-element.1213), channel_id=1, source_target_pairs={{0,1},{1,0},{2,3},{3,2},{4,5},{5,4},{6,7},{7,6},{8,9},{9,8},{10,11... | collective-permute-start | bytes 20744 | tf_op jit(solution)/shard_map/while/body/eval_jaxpr/ppermute | solution.py:23
  110.6 1.5 collective-permute-start
  110.6 3.2 collective-permute-start.1
  114.7 8.7 %collective-permute-start.2 = (f32[3,144,4]{2,1,0:T(8,128)}, f32[3,144,4]{2,1,0:T(8,128)}, u32[]{:S(2)}, u32[]{:S(2)}) collective-permute-start(f32[3,144,4]{2,1,0:T(8,128)} %get-tuple-element.1212), channel_id=1, source_target_pairs={{1,0},{0,1},{3,2},{2,3},{5,4},{4,5},{7,6},{6,7},{9,8},{8,9},{11,10... | collective-permute-start | bytes 20744 | tf_op jit(solution)/shard_map/while/body/eval_jaxpr/ppermute | solution.py:26
  116.4 10.1 %collective-permute-start.3 = (f32[3,144,4]{2,1,0:T(8,128)}, f32[3,144,4]{2,1,0:T(8,128)}, u32[]{:S(2)}, u32[]{:S(2)}) collective-permute-start(f32[3,144,4]{2,1,0:T(8,128)} %get-tuple-element.1213), channel_id=1, source_target_pairs={{0,1},{1,0},{2,3},{3,2},{4,5},{5,4},{6,7},{7,6},{8,9},{9,8},{10,11... | collective-permute-start | bytes 20744 | tf_op jit(solution)/shard_map/while/body/eval_jaxpr/ppermute | solution.py:23
  134.1 17.0 %collective-permute-start.14 = (f32[3,136,384]{2,1,0:T(8,128)S(1)}, f32[3,136,384]{2,1,0:T(8,128)}, u32[]{:S(2)}, u32[]{:S(2)}) collective-permute-start(f32[3,136,384]{2,1,0:T(8,128)S(1)} %get-tuple-element.781), channel_id=1, source_target_pairs={{0,8},{8,16},{16,24},{24,0},{1,9},{9,17},{17,25},{25,1},{2,10},{10... | collective-permute-start | bytes 1880072 | tf_op jit(solution)/shard_map/ppermute | solution.py:34
  136.2 15.0 %copy-start.9 = (f32[1,3,136,384]{3,2,1,0:T(8,128)S(1)}, f32[1,3,136,384]{3,2,1,0:T(8,128)}, u32[]{:S(2)}) copy-start(f32[1,3,136,384]{3,2,1,0:T(8,128)} %param.21) | copy-start | bytes 1880068
  151.2 2.3 copy-start
  152.4 1.1 copy-start.2
  153.5 13.3 %collective-permute-start.4 = (f32[3,136,384]{2,1,0:T(8,128)}, f32[3,136,384]{2,1,0:T(8,128)}, u32[]{:S(2)}, u32[]{:S(2)}) collective-permute-start(f32[3,136,384]{2,1,0:T(8,128)} %get-tuple-element.1340), channel_id=1, source_target_pairs={{0,8},{8,16},{16,24},{1,9},{9,17},{17,25},{2,10},{10,18},{18,26},{... | collective-permute-start | bytes 1880072 | tf_op jit(solution)/shard_map/while/body/eval_jaxpr/ppermute | solution.py:40
  169.1 15.2 %collective-permute-start.4 = (f32[3,136,384]{2,1,0:T(8,128)}, f32[3,136,384]{2,1,0:T(8,128)}, u32[]{:S(2)}, u32[]{:S(2)}) collective-permute-start(f32[3,136,384]{2,1,0:T(8,128)} %get-tuple-element.1340), channel_id=1, source_target_pairs={{0,8},{8,16},{16,24},{1,9},{9,17},{17,25},{2,10},{10,18},{18,26},{... | collective-permute-start | bytes 1880072 | tf_op jit(solution)/shard_map/while/body/eval_jaxpr/ppermute | solution.py:40
  186.4 14.3 %collective-permute-start.4 = (f32[3,136,384]{2,1,0:T(8,128)}, f32[3,136,384]{2,1,0:T(8,128)}, u32[]{:S(2)}, u32[]{:S(2)}) collective-permute-start(f32[3,136,384]{2,1,0:T(8,128)} %get-tuple-element.1340), channel_id=1, source_target_pairs={{0,8},{8,16},{16,24},{1,9},{9,17},{17,25},{2,10},{10,18},{18,26},{... | collective-permute-start | bytes 1880072 | tf_op jit(solution)/shard_map/while/body/eval_jaxpr/ppermute | solution.py:40
  205.1 1.5 collective-permute-start.6
  205.2 3.2 collective-permute-start.7
  209.3 8.5 %collective-permute-start.8 = (f32[3,144,4]{2,1,0:T(8,128)}, f32[3,144,4]{2,1,0:T(8,128)}, u32[]{:S(2)}, u32[]{:S(2)}) collective-permute-start(f32[3,144,4]{2,1,0:T(8,128)} %get-tuple-element.1260), channel_id=1, source_target_pairs={{1,0},{0,1},{3,2},{2,3},{5,4},{4,5},{7,6},{6,7},{9,8},{8,9},{11,10... | collective-permute-start | bytes 20744 | tf_op jit(solution)/shard_map/while/body/eval_jaxpr/ppermute | solution.py:26
  210.1 10.0 %collective-permute-start.9 = (f32[3,144,4]{2,1,0:T(8,128)}, f32[3,144,4]{2,1,0:T(8,128)}, u32[]{:S(2)}, u32[]{:S(2)}) collective-permute-start(f32[3,144,4]{2,1,0:T(8,128)} %get-tuple-element.1261), channel_id=1, source_target_pairs={{0,1},{1,0},{2,3},{3,2},{4,5},{5,4},{6,7},{7,6},{8,9},{9,8},{10,11... | collective-permute-start | bytes 20744 | tf_op jit(solution)/shard_map/while/body/eval_jaxpr/ppermute | solution.py:23
  227.3 1.2 copy-start.3
  227.3 1.2 copy-start.6
  230.0 2.4 collective-permute-start.6
  231.0 3.2 collective-permute-start.7
  235.0 8.7 %collective-permute-start.8 = (f32[3,144,4]{2,1,0:T(8,128)}, f32[3,144,4]{2,1,0:T(8,128)}, u32[]{:S(2)}, u32[]{:S(2)}) collective-permute-start(f32[3,144,4]{2,1,0:T(8,128)} %get-tuple-element.1260), channel_id=1, source_target_pairs={{1,0},{0,1},{3,2},{2,3},{5,4},{4,5},{7,6},{6,7},{9,8},{8,9},{11,10... | collective-permute-start | bytes 20744 | tf_op jit(solution)/shard_map/while/body/eval_jaxpr/ppermute | solution.py:26
  235.9 11.0 %collective-permute-start.9 = (f32[3,144,4]{2,1,0:T(8,128)}, f32[3,144,4]{2,1,0:T(8,128)}, u32[]{:S(2)}, u32[]{:S(2)}) collective-permute-start(f32[3,144,4]{2,1,0:T(8,128)} %get-tuple-element.1261), channel_id=1, source_target_pairs={{0,1},{1,0},{2,3},{3,2},{4,5},{5,4},{6,7},{7,6},{8,9},{9,8},{10,11... | collective-permute-start | bytes 20744 | tf_op jit(solution)/shard_map/while/body/eval_jaxpr/ppermute | solution.py:23
  254.1 1.2 copy-start.3
  254.1 1.2 copy-start.6
  256.8 1.5 collective-permute-start.6
  256.8 3.2 collective-permute-start.7
  260.9 8.7 %collective-permute-start.8 = (f32[3,144,4]{2,1,0:T(8,128)}, f32[3,144,4]{2,1,0:T(8,128)}, u32[]{:S(2)}, u32[]{:S(2)}) collective-permute-start(f32[3,144,4]{2,1,0:T(8,128)} %get-tuple-element.1260), channel_id=1, source_target_pairs={{1,0},{0,1},{3,2},{2,3},{5,4},{4,5},{7,6},{6,7},{9,8},{8,9},{11,10... | collective-permute-start | bytes 20744 | tf_op jit(solution)/shard_map/while/body/eval_jaxpr/ppermute | solution.py:26
  261.8 10.8 %collective-permute-start.9 = (f32[3,144,4]{2,1,0:T(8,128)}, f32[3,144,4]{2,1,0:T(8,128)}, u32[]{:S(2)}, u32[]{:S(2)}) collective-permute-start(f32[3,144,4]{2,1,0:T(8,128)} %get-tuple-element.1261), channel_id=1, source_target_pairs={{0,1},{1,0},{2,3},{3,2},{4,5},{5,4},{6,7},{7,6},{8,9},{9,8},{10,11... | collective-permute-start | bytes 20744 | tf_op jit(solution)/shard_map/while/body/eval_jaxpr/ppermute | solution.py:23
  279.7 1.2 copy-start.3
  279.7 1.2 copy-start.6
  282.4 1.5 collective-permute-start.6
  282.5 3.2 collective-permute-start.7
  286.6 8.7 %collective-permute-start.8 = (f32[3,144,4]{2,1,0:T(8,128)}, f32[3,144,4]{2,1,0:T(8,128)}, u32[]{:S(2)}, u32[]{:S(2)}) collective-permute-start(f32[3,144,4]{2,1,0:T(8,128)} %get-tuple-element.1260), channel_id=1, source_target_pairs={{1,0},{0,1},{3,2},{2,3},{5,4},{4,5},{7,6},{6,7},{9,8},{8,9},{11,10... | collective-permute-start | bytes 20744 | tf_op jit(solution)/shard_map/while/body/eval_jaxpr/ppermute | solution.py:26
  287.4 11.0 %collective-permute-start.9 = (f32[3,144,4]{2,1,0:T(8,128)}, f32[3,144,4]{2,1,0:T(8,128)}, u32[]{:S(2)}, u32[]{:S(2)}) collective-permute-start(f32[3,144,4]{2,1,0:T(8,128)} %get-tuple-element.1261), channel_id=1, source_target_pairs={{0,1},{1,0},{2,3},{3,2},{4,5},{5,4},{6,7},{7,6},{8,9},{9,8},{10,11... | collective-permute-start | bytes 20744 | tf_op jit(solution)/shard_map/while/body/eval_jaxpr/ppermute | solution.py:23
  305.6 1.2 copy-start.3
  305.6 1.2 copy-start.6
  308.3 41.6 %collective-permute-start.15 = (f32[3,136,384]{2,1,0:T(8,128)S(1)}, f32[3,136,384]{2,1,0:T(8,128)S(1)}, u32[]{:S(2)}, u32[]{:S(2)}) collective-permute-start(f32[3,136,384]{2,1,0:T(8,128)S(1)} %get-tuple-element.783), channel_id=1, source_target_pairs={{0,8},{8,16},{16,24},{24,0},{1,9},{9,17},{17,25},{25,1},{2,10},{10... | collective-permute-start | bytes 1880072 | tf_op jit(solution)/shard_map/ppermute | solution.py:34
  349.9 1.3 copy-start.1
  351.1 44.9 %copy-start.5 = (f32[3,136,384]{2,1,0:T(8,128)S(1)}, f32[3,136,384]{2,1,0:T(8,128)}, u32[]{:S(2)}) copy-start(f32[3,136,384]{2,1,0:T(8,128)} %copy-done.4) | copy-start | bytes 1880068
  351.2 15.4 %collective-permute-start.5 = (f32[3,136,384]{2,1,0:T(8,128)S(1)}, f32[3,136,384]{2,1,0:T(8,128)S(1)}, u32[]{:S(2)}, u32[]{:S(2)}) collective-permute-start(f32[3,136,384]{2,1,0:T(8,128)S(1)} %get-tuple-element.1418), channel_id=1, source_target_pairs={{0,8},{8,16},{16,24},{1,9},{9,17},{17,25},{2,10},{10,18},{18,26},{... | collective-permute-start | bytes 1880072 | tf_op jit(solution)/shard_map/while/body/eval_jaxpr/ppermute | solution.py:40
  366.7 15.0 %collective-permute-start.5 = (f32[3,136,384]{2,1,0:T(8,128)S(1)}, f32[3,136,384]{2,1,0:T(8,128)S(1)}, u32[]{:S(2)}, u32[]{:S(2)}) collective-permute-start(f32[3,136,384]{2,1,0:T(8,128)S(1)} %get-tuple-element.1418), channel_id=1, source_target_pairs={{0,8},{8,16},{16,24},{1,9},{9,17},{17,25},{2,10},{10,18},{18,26},{... | collective-permute-start | bytes 1880072 | tf_op jit(solution)/shard_map/while/body/eval_jaxpr/ppermute | solution.py:40
  381.9 14.1 %collective-permute-start.5 = (f32[3,136,384]{2,1,0:T(8,128)S(1)}, f32[3,136,384]{2,1,0:T(8,128)S(1)}, u32[]{:S(2)}, u32[]{:S(2)}) collective-permute-start(f32[3,136,384]{2,1,0:T(8,128)S(1)} %get-tuple-element.1418), channel_id=1, source_target_pairs={{0,8},{8,16},{16,24},{1,9},{9,17},{17,25},{2,10},{10,18},{18,26},{... | collective-permute-start | bytes 1880072 | tf_op jit(solution)/shard_map/while/body/eval_jaxpr/ppermute | solution.py:40
  (5 other events, 3.7 us)
Sparse Core Ops, SparseCore 0:
  310.9 37.2 all-reduce.1
where the time goes:
time: 405 us; the launch traced here: 404 us
  waiting for transfers between devices  225 us (56%)
  other arithmetic  93.2 us (23%)
  starting transfers between devices  56.7 us (14%)
  between operations  14.2 us (4%)
  local copies, waits for them, and re-layouts  8.55 us (2%)
  loops' own time  5.87 us (1%)
    ppermute x18, waiting for transfers between devices, padded_2(): lax.ppermute(lax.slice_in_dim(block, 0, width, axis=dim), axis, backward)  65.5 us
    ppermute x6, waiting for transfers between devices, shifted_2(): return lax.ppermute(block, axis, route)  61.5 us
    ppermute x18, waiting for transfers between devices, padded_2(): lax.ppermute(lax.slice_in_dim(block, block.shape[dim] - width, None, axis...  49.1 us
    psum x1, waiting for transfers between devices, shards(): summed = lax.psum(total, 'tm')  37.4 us
    ppermute x6, starting transfers between devices, shifted_2(): return lax.ppermute(block, axis, route)  25.7 us
    mul x32, other arithmetic, advance(): flux_v = depth_v[1:, 1:-1] * merid_new  17.7 us
    mul x32, other arithmetic, advance(): flux_u = depth_u[1:-1, 1:] * zonal_new  16 us
    ppermute x18, starting transfers between devices, padded_2(): lax.ppermute(lax.slice_in_dim(block, 0, width, axis=dim), axis, backward)  15.6 us
  transfers between devices with their start and end apart: 45, of which 44 were waited for; matrix products, arithmetic and copies ran while one was open for 1% of the time, Pallas kernels for 0%

commit v1 on v0

v1 whole, which is shorter than its diff:
```python
import functools
import math

import jax
import jax.numpy as jnp
import numpy as np
from jax import lax
from jax.experimental import pallas as pl
from jax.experimental.pallas import tpu as pltpu
from jax.sharding import PartitionSpec as P

STEPS = 16
SWEEPS = 2
DCLASS = 32
WIDE = STEPS
LANES = 128
TILE = 8
SKEW = 2

MESH = pl.DeviceIdType.MESH


def kernel(
    sizes, cls_ref, ocean_ref, lev_ref, drag_ref, force_ref, flow_ref, guess_ref, trig_ref,
    out_ref, grad_ref,
    x_ref, y_ref, st_ref, acc_ref, gain_ref, old_ref, term_ref, east_out, west_out, east_in, west_in,
    c1_ref, cs1_ref, e1_ref, c2_ref, cs2_ref, e2_ref, tot_ref,
    row_send, row_recv, col_send, col_recv,
    c_send, c_recv, e_send, e_recv, t_send, t_recv,
):
    n, n_lat, n_lon = sizes
    rows, cols = ocean_ref.shape
    high, wid = x_ref.shape[1], x_ref.shape[2]
    span = c1_ref.shape[2]
    block = TILE * max(d for d in (1, 2, 3) if (high // TILE) % d == 0)
    count = rows // TILE
    k, lat, lon = lax.axis_index("tm"), lax.axis_index("lat"), lax.axis_index("lon")
    north, south = lax.rem(lat + 1, n_lat), lax.rem(lat + n_lat - 1, n_lat)
    east, west = lax.rem(lon + 1, n_lon), lax.rem(lon + n_lon - 1, n_lon)
    later, sooner = lax.rem(k + 1, n), lax.rem(k + n - 1, n)

    barrier = pltpu.get_barrier_semaphore()
    for axis, spot in (
        ("lat", north), ("lat", south), ("lon", east), ("lon", west), ("tm", later), ("tm", sooner)
    ):
        pl.semaphore_signal(barrier, inc=1, device_id={axis: spot}, device_id_type=MESH)

    mine = pl.ds(WIDE, rows)
    classes = cls_ref[...]
    depth = jnp.zeros((rows, cols), jnp.float32)
    for c in range(DCLASS):
        depth = jnp.where(classes == c, lev_ref[c], depth)
    x_ref[0, mine, :cols] = depth
    line = lat * rows + lax.broadcasted_iota(jnp.int32, (rows, cols), 0)
    polar = (line == 0) | (line == n_lat * rows - 1)
    x_ref[1, mine, :cols] = jnp.where(polar, 0, ocean_ref[...]).astype(jnp.float32)
    x_ref[2, mine, :cols] = drag_ref[...]
    for f in range(2):
        x_ref[3 + f, mine, :cols] = force_ref[f]
    for f in range(3):
        x_ref[5 + f, mine, :cols] = guess_ref[0, f]
    pl.semaphore_wait(barrier, 6)

    def exchange(ref, number, fills):
        fields = len(fills)
        up = pltpu.make_async_remote_copy(
            src_ref=ref.at[:, pl.ds(rows, WIDE), pl.ds(0, span)],
            dst_ref=ref.at[:, pl.ds(0, WIDE), pl.ds(0, span)],
            send_sem=row_send.at[2 * number], recv_sem=row_recv.at[2 * number],
            device_id={"lat": north}, device_id_type=MESH,
        )
        down = pltpu.make_async_remote_copy(
            src_ref=ref.at[:, pl.ds(WIDE, WIDE), pl.ds(0, span)],
            dst_ref=ref.at[:, pl.ds(WIDE + rows, WIDE), pl.ds(0, span)],
            send_sem=row_send.at[2 * number + 1], recv_sem=row_recv.at[2 * number + 1],
            device_id={"lat": south}, device_id_type=MESH,
        )
        up.start()
        down.start()
        up.wait()
        down.wait()
        lane = lax.broadcasted_iota(jnp.int32, (high, LANES), 1)
        last = (cols - WIDE) // LANES * LANES
        inset = cols - WIDE - last
        eastern = western = None
        for f in range(fields):
            e = pltpu.roll(ref[f, :, last : last + LANES], (WIDE * f - inset) % LANES, 1)
            w = pltpu.roll(ref[f, :, :LANES], WIDE * f, 1) if f else ref[f, :, :LANES]
            eastern = jnp.where(lane >= WIDE * f, e, eastern) if f else e
            western = jnp.where(lane >= WIDE * f, w, western) if f else w
        east_out[number] = eastern
        west_out[number] = western
        right = pltpu.make_async_remote_copy(
            src_ref=east_out.at[number], dst_ref=west_in.at[number],
            send_sem=col_send.at[2 * number], recv_sem=col_recv.at[2 * number],
            device_id={"lon": east}, device_id_type=MESH,
        )
        left = pltpu.make_async_remote_copy(
            src_ref=west_out.at[number], dst_ref=east_in.at[number],
            send_sem=col_send.at[2 * number + 1], recv_sem=col_recv.at[2 * number + 1],
            device_id={"lon": west}, device_id_type=MESH,
        )
        right.start()
        left.start()
        right.wait()
        left.wait()
        start = wid - LANES
        own = cols - start
        from_east, from_west = east_in[number], west_in[number]
        for f, fill in enumerate(fills):
            e = pltpu.roll(from_east, (own - WIDE * f) % LANES, 1)
            w = pltpu.roll(from_west, (LANES - WIDE - WIDE * f) % LANES, 1)
            halo = jnp.where(lane < own + WIDE, e, jnp.where(lane >= LANES - WIDE, w, fill))
            if own:
                halo = jnp.where(lane < own, ref[f, :, start:], halo)
            ref[f, :, start:] = halo

    exchange(x_ref, 0, (1.0,) + (0.0,) * 7)

    def below(ref, f, r):
        if r == 0:
            return pltpu.roll(ref[f, :block, :], 1, 0)
        return pltpu.roll(ref[f, r - TILE : r + block, :], 1, 0)[TILE:]

    for r in range(0, high, block):
        here = pl.ds(r, block)
        d, m, g = x_ref[0, here, :], x_ref[1, here, :], x_ref[2, here, :]
        for side, shifted in enumerate(
            (lambda f, v: pltpu.roll(v, 1, 1), lambda f, v: below(x_ref, f, r))
        ):
            both = d + shifted(0, d)
            wet = m * shifted(1, m)
            st_ref[side, here, :] = wet * (1.0 - (g + shifted(2, g)) / both)
            st_ref[2 + side, here, :] = 0.7 * wet
            st_ref[4 + side, here, :] = 0.3 * both
        st_ref[6, here, :] = m
        st_ref[7, here, :] = m * x_ref[3, here, :]
        st_ref[8, here, :] = m * x_ref[4, here, :]
    gain_ref[0] = x_ref[1, mine, :span]
    for side in range(2):
        g = st_ref[side, mine, :span]
        for _ in range(STEPS.bit_length() - 1):
            g = g * g
        gain_ref[1 + side] = g
    acc_ref[...] = jnp.zeros(acc_ref.shape, jnp.float32)

    def sweep(ref, base, want):
        def step(t, nothing):
            cosine = trig_ref[2 * (k * STEPS + t)]
            sine = trig_ref[2 * (k * STEPS + t) + 1]
            carry = None
            for r in reversed(range(0, high, block)):
                here = pl.ds(r, block)
                a = ref[base, here, :]
                p = st_ref[0, here, :] * ref[base + 1, here, :] - st_ref[2, here, :] * (
                    a - pltpu.roll(a, 1, 1)
                )
                q = st_ref[1, here, :] * ref[base + 2, here, :] - st_ref[3, here, :] * (
                    a - below(ref, base, r)
                )
                u = st_ref[4, here, :] * p
                v = st_ref[5, here, :] * q
                if carry is None:
                    v_north = pltpu.roll(v, block - 1, 0)
                else:
                    v_north = pltpu.roll(
                        jnp.concatenate([v, carry], axis=0), block + TILE - 1, 0
                    )[:block]
                carry = v[:TILE]
                spread = (pltpu.roll(u, wid - 1, 1) - u) + (v_north - v)
                ref[base, here, :] = st_ref[6, here, :] * (a - spread) + (
                    st_ref[7, here, :] * cosine + st_ref[8, here, :] * sine
                )
                ref[base + 1, here, :] = p
                ref[base + 2, here, :] = q
                if want:
                    low, top = max(r, WIDE), min(r + block, WIDE + rows + TILE)
                    part = pl.ds(low, top - low)
                    p, q = p[low - r : top - r], q[low - r : top - r]
                    acc_ref[0, part, :] += cosine * p
                    acc_ref[1, part, :] += sine * p
                    acc_ref[2, part, :] += cosine * q
                    acc_ref[3, part, :] += sine * q
            return nothing

        lax.fori_loop(0, STEPS, step, 0)

    def relay(ref, base, number, c_ref, cs_ref, e_ref, want):
        def piece(chunk):
            return pl.ds(pl.multiple_of(chunk * TILE, TILE), TILE)

        def forward(chunk):
            return pltpu.make_async_remote_copy(
                src_ref=cs_ref.at[:, piece(chunk)], dst_ref=c_ref.at[:, piece(chunk)],
                send_sem=c_send.at[number, chunk], recv_sem=c_recv.at[number, chunk],
                device_id={"tm": later}, device_id_type=MESH,
            )

        def back(chunk):
            return pltpu.make_async_remote_copy(
                src_ref=e_ref.at[:, piece(chunk)], dst_ref=e_ref.at[:, piece(chunk)],
                send_sem=e_send.at[number, chunk], recv_sem=e_recv.at[number, chunk],
                device_id={"tm": sooner}, device_id_type=MESH,
            )

        def total(chunk):
            return pltpu.make_async_remote_copy(
                src_ref=tot_ref.at[piece(chunk)], dst_ref=tot_ref.at[piece(chunk)],
                send_sem=t_send.at[chunk], recv_sem=t_recv.at[chunk],
                device_id={"tm": sooner}, device_id_type=MESH,
            )

        @pl.when(k == 0)
        def _():
            c_ref[...] = jnp.zeros(c_ref.shape, jnp.float32)

        @pl.when(k == n - 1)
        def _():
            for f in range(3):
                e_ref[f] = ref[base + f, mine, :span]

        def turn(i, nothing):
            ahead = i - SKEW * k

            @pl.when((ahead >= 0) & (ahead < count))
            def _():
                @pl.when(k > 0)
                def _():
                    forward(ahead).wait_recv()

                here = piece(ahead)
                there = pl.ds(pl.multiple_of(WIDE + ahead * TILE, TILE), TILE)

                @pl.when(k < n - 1)
                def _():
                    for f in range(3):
                        cs_ref[f, here, :] = ref[base + f, there, :span] + gain_ref[f, here, :] * (
                            c_ref[f, here, :] - old_ref[f, here, :]
                        )
                    if want:
                        cs_ref[3, here, :] = c_ref[3, here, :] + term_ref[here, :]
                    forward(ahead).start()

                if want:
                    @pl.when(k == n - 1)
                    def _():
                        tot_ref[here, :] = c_ref[3, here, :] + term_ref[here, :]

            behind = i - SKEW * (n - 1 - k)

            @pl.when((behind >= 0) & (behind < count))
            def _():
                @pl.when(k < n - 1)
                def _():
                    back(behind).wait_recv()

                @pl.when(k > 0)
                def _():
                    back(behind).start()

            if want:
                final = behind - SKEW * (n - 1)

                @pl.when((final >= 0) & (final < count))
                def _():
                    @pl.when(k < n - 1)
                    def _():
                        total(final).wait_recv()

                    @pl.when(k > 0)
                    def _():
                        total(final).start()

            return nothing

        lax.fori_loop(0, count + SKEW * (n - 1) * (2 if want else 1), turn, 0)

        for f in range(3):
            power = e_ref[f]
            for j in range(n - 1):
                power = power * jnp.where(j < k, gain_ref[f], 1.0)
            fresh = c_ref[f] + power
            if want:
                out_ref[0, f] = fresh[:, :cols]
            else:
                old_ref[f] = fresh
                y_ref[f, mine, :span] = fresh

        def sent(chunk, nothing):
            @pl.when(k < n - 1)
            def _():
                forward(chunk).wait_send()

            @pl.when(k > 0)
            def _():
                back(chunk).wait_send()
                if want:
                    total(chunk).wait_send()

            return nothing

        return lambda: lax.fori_loop(0, count, sent, 0)

    for f in range(3):
        old_ref[f] = x_ref[5 + f, mine, :span]
    sweep(x_ref, 5, False)
    finish_first = relay(x_ref, 5, 0, c1_ref, cs1_ref, e1_ref, False)
    exchange(y_ref, 1, (0.0,) * 3)
    sweep(y_ref, 0, True)

    weight = 0.5 * x_ref[1, mine, :span] / x_ref[0, mine, :span]
    term = jnp.zeros((rows, span), jnp.float32)
    for f in range(4):
        if f < 2:
            v = acc_ref[f, mine, :]
            mid = (v + pltpu.roll(v, wid - 1, 1))[:, :span]
        else:
            v = acc_ref[f, pl.ds(WIDE, rows + TILE), :span]
            mid = (v + pltpu.roll(v, rows + TILE - 1, 0))[:rows]
        flow = flow_ref[f]
        if span > cols:
            flow = jnp.concatenate([flow, jnp.zeros((rows, span - cols), jnp.float32)], axis=1)
        term = term + flow * mid
    term_ref[...] = weight * term

    finish_second = relay(y_ref, 0, 1, c2_ref, cs2_ref, e2_ref, True)
    grad_ref[...] = tot_ref[:, :cols] * (1.0 / (n * STEPS))
    finish_first()
    finish_second()


def shards(
    sizes, depth_class, ocean_mask, depth_levels, drag, tide_force, forward_flow, guess
):
    n = sizes[0]
    rows, cols = ocean_mask.shape
    high = rows + 2 * WIDE
    wid = -(-(cols + 2 * WIDE) // LANES) * LANES
    span = -(-cols // LANES) * LANES
    count = rows // TILE
    assert rows % TILE == 0 and rows >= WIDE and wid - LANES <= cols
    counts = np.arange(1, n * STEPS + 1)
    angle = 2.0 * math.pi * counts / (n * STEPS)
    trig = jnp.asarray(np.stack([np.cos(angle), np.sin(angle)], axis=1).reshape(-1), jnp.float32)
    f32 = jnp.float32
    vmem, smem = pl.BlockSpec(memory_space=pltpu.VMEM), pl.BlockSpec(memory_space=pltpu.SMEM)
    dma = pltpu.SemaphoreType.DMA
    return pl.pallas_call(
        functools.partial(kernel, sizes),
        out_shape=(
            jax.ShapeDtypeStruct((1, 3, rows, cols), f32),
            jax.ShapeDtypeStruct((rows, cols), f32),
        ),
        in_specs=[vmem, vmem, smem, vmem, vmem, vmem, vmem, smem],
        out_specs=(vmem, vmem),
        scratch_shapes=[
            pltpu.VMEM((8, high, wid), f32),
            pltpu.VMEM((3, high, wid), f32),
            pltpu.VMEM((9, high, wid), f32),
            pltpu.VMEM((4, high, wid), f32),
            pltpu.VMEM((3, rows, span), f32),
            pltpu.VMEM((3, rows, span), f32),
            pltpu.VMEM((rows, span), f32),
            pltpu.VMEM((2, high, LANES), f32),
            pltpu.VMEM((2, high, LANES), f32),
            pltpu.VMEM((2, high, LANES), f32),
            pltpu.VMEM((2, high, LANES), f32),
            pltpu.VMEM((3, rows, span), f32),
            pltpu.VMEM((3, rows, span), f32),
            pltpu.VMEM((3, rows, span), f32),
            pltpu.VMEM((4, rows, span), f32),
            pltpu.VMEM((4, rows, span), f32),
            pltpu.VMEM((3, rows, span), f32),
            pltpu.VMEM((rows, span), f32),
            dma((4,)), dma((4,)), dma((4,)), dma((4,)),
            dma((2, count)), dma((2, count)), dma((2, count)), dma((2, count)),
            dma((count,)), dma((count,)),
        ],
        compiler_params=pltpu.CompilerParams(
            collective_id=0, has_side_effects=True, vmem_limit_bytes=40 * 1024 * 1024
        ),
        name="parareal",
    )(depth_class, ocean_mask, depth_levels, drag, tide_force, forward_flow, guess, trig)


def solution(mesh):
    sizes = tuple(mesh.shape[axis] for axis in ("tm", "lat", "lon"))
    return jax.shard_map(
        functools.partial(shards, sizes),
        mesh=mesh,
        in_specs=(
            P("lat", "lon"),
            P("lat", "lon"),
            P(),
            P("lat", "lon"),
            P(None, "lat", "lon"),
            P(None, "lat", "lon"),
            P("tm", None, "lat", "lon"),
        ),
        out_specs=(P("tm", None, "lat", "lon"), P("lat", "lon")),
        check_vma=False,
    )
```

time: 405 us -> 126 us (0.31)
  waiting for transfers between devices: 225 us -> 0 us
  Pallas kernels: 0 us -> 117 us
  other arithmetic: 93.2 us -> 0 us
  starting transfers between devices: 56.7 us -> 0 us
  between operations: 14.2 us -> 0.66 us
  loops' own time: 5.87 us -> 0 us
    ppermute x44 -> x0, waiting for transfers between devices: 188 us -> none  [the longest x18 65.5 us: padded_2(): lax.ppermute(lax.slice_in_dim(block, 0, width, axis=dim), axis, backward)]
    pallas_call x0 -> x1, Pallas kernels: none -> 117 us  [shards(): pl.pallas_call(functools.partial(kernel, sizes), out_shape=(jax.ShapeDtyp...]
    ppermute x44 -> x0, starting transfers between devices: 56.7 us -> none  [the longest x6 25.7 us: shifted_2(): return lax.ppermute(block, axis, route)]
    mul x89 -> x0, other arithmetic: 45.2 us -> none  [the longest x32 17.7 us: advance(): flux_v = depth_v[1:, 1:-1] * merid_new]
    psum x1 -> x0, waiting for transfers between devices: 37.4 us -> none  [shards(): summed = lax.psum(total, 'tm')]
    concatenate x9 -> x0, other arithmetic: 12.9 us -> none  [padded_2(): block = jnp.concatenate([low, block, high], axis=dim)]
    add x11 -> x0, other arithmetic: 11.6 us -> none  [the longest x6 7.02 us: relay(): return jump + gain * shifted_2(change_now, 'tm', 1)]
    slice x10 -> x0, other arithmetic: 8.53 us -> none  [padded_2(): lax.slice_in_dim(block, block.shape[dim] - width, None, axis=dim)]
  transfers between devices with their start and end apart: 45 -> 0, of which waited for: 44 -> 0; matrix products, arithmetic and copies ran while one was open for 1% -> 0% of each run, Pallas kernels for 0% -> 0%
where the time goes in v1:
time: 126 us
  Pallas kernels  117 us (93%)
  local copies, waits for them, and re-layouts  8.84 us (7%)
    pallas_call x1, Pallas kernels, shards(): pl.pallas_call(functools.partial(kernel, sizes), out_shape=(jax.ShapeDtyp...  117 us
    unnamed x18, local copies, waits for them, and re-layouts  8.84 us

profile of v1, /device:TPU:0, one launch (start us, length us, event | category | flops | bytes accessed | tf_op | source)
XLA Modules:
  0.0 126.1 jit_solution(12387357445561558106)
XLA Ops:
  0.6 0.0 copy-start
  0.6 1.1 copy-done
  1.8 0.0 copy-start.1
  1.8 1.1 copy-done.1
  2.9 0.0 copy-start.2
  2.9 1.0 copy-done.2
  3.9 0.0 copy-start.3
  3.9 0.9 copy-done.3
  4.8 0.0 copy-start.4
  4.8 0.9 copy-done.4
  5.7 0.0 copy-start.5
  5.7 0.9 copy-done.5
  6.7 0.0 copy-start.6
  6.7 0.7 copy-done.6
  7.3 0.0 copy-start.7
  7.3 0.7 copy-done.7
  8.0 116.6 %parareal.1 = (f32[1,3,136,384]{3,2,1,0:T(8,128)S(1)}, f32[136,384]{1,0:T(8,128)S(1)}) custom-call(s32[136,384]{1,0:T(8,128)S(1)} %copy-done.3, s32[136,384]{1,0:T(8,128)S(1)} %copy-done.4, f32[32]{0:T(128)S(1)} %copy-done.6, f32[136,384]{1,0:T(8,128)S(1)} %copy-done.5, f32[2,136,384]{2,1,0:T(8,128)S(1)} %copy-done.2, f32[4,136,384]{2,1,0:T(8,128)S(1)} %copy-done, ...), custom_call_target="tpu_custom_call" | custom-call | tf_op jit(solution)/shard_map/parareal/pallas_call | solution.py:348
  124.6 0.8 copy.12
  125.4 0.7 copy.13
Async XLA Ops:
  0.6 1.2 copy-start
  1.8 1.1 copy-start.1
  2.9 1.0 copy-start.2
  3.9 0.9 copy-start.3
  4.8 0.9 copy-start.4
  5.7 0.9 copy-start.5
  6.7 0.7 copy-start.6
  7.3 0.7 copy-start.7

commit v2 on v1

--- a/solution.py
+++ b/solution.py
@@ -15,16 +15,17 @@
 WIDE = STEPS
 LANES = 128
 TILE = 8
-SKEW = 2
+SKEW = 4
 
 MESH = pl.DeviceIdType.MESH
 
 
 def kernel(
-    sizes, cls_ref, ocean_ref, lev_ref, drag_ref, force_ref, flow_ref, guess_ref, trig_ref,
+    sizes, cls_hbm, ocean_hbm, lev_hbm, drag_hbm, force_hbm, flow_hbm, guess_hbm, trig_hbm,
     out_ref, grad_ref,
+    cls_ref, ocean_ref, lev_ref, drag_ref, force_ref, flow_ref, guess_ref, trig_ref, load_sem,
     x_ref, y_ref, st_ref, acc_ref, gain_ref, old_ref, term_ref, east_out, west_out, east_in, west_in,
-    c1_ref, cs1_ref, e1_ref, c2_ref, cs2_ref, e2_ref, tot_ref,
+    c1_ref, cs1_ref, e1_ref, c2_ref, cs2_ref, e2_ref, part_ref, other_ref, tot_ref,
     row_send, row_recv, col_send, col_recv,
     c_send, c_recv, e_send, e_recv, t_send, t_recv,
 ):
@@ -39,6 +40,15 @@
     east, west = lax.rem(lon + 1, n_lon), lax.rem(lon + n_lon - 1, n_lon)
     later, sooner = lax.rem(k + 1, n), lax.rem(k + n - 1, n)
 
+    loads = [
+        pltpu.make_async_copy(source, target, load_sem.at[i])
+        for i, (source, target) in enumerate((
+            (lev_hbm, lev_ref), (cls_hbm, cls_ref), (ocean_hbm, ocean_ref), (drag_hbm, drag_ref),
+            (force_hbm, force_ref), (guess_hbm, guess_ref), (trig_hbm, trig_ref), (flow_hbm, flow_ref),
+        ))
+    ]
+    for load in loads:
+        load.start()
     barrier = pltpu.get_barrier_semaphore()
     for axis, spot in (
         ("lat", north), ("lat", south), ("lon", east), ("lon", west), ("tm", later), ("tm", sooner)
@@ -46,11 +56,15 @@
         pl.semaphore_signal(barrier, inc=1, device_id={axis: spot}, device_id_type=MESH)
 
     mine = pl.ds(WIDE, rows)
+    loads[0].wait()
+    loads[1].wait()
     classes = cls_ref[...]
     depth = jnp.zeros((rows, cols), jnp.float32)
     for c in range(DCLASS):
         depth = jnp.where(classes == c, lev_ref[c], depth)
     x_ref[0, mine, :cols] = depth
+    for load in loads[2:7]:
+        load.wait()
     line = lat * rows + lax.broadcasted_iota(jnp.int32, (rows, cols), 0)
     polar = (line == 0) | (line == n_lat * rows - 1)
     x_ref[1, mine, :cols] = jnp.where(polar, 0, ocean_ref[...]).astype(jnp.float32)
@@ -185,6 +199,69 @@
 
         lax.fori_loop(0, STEPS, step, 0)
 
+    half = n // 2
+    place = jnp.where(k < half, k, n - 1 - k)
+    inner, outer = jnp.where(k < half, later, sooner), jnp.where(k < half, sooner, later)
+
+    def gather():
+        return pltpu.make_async_remote_copy(
+            src_ref=term_ref, dst_ref=part_ref, send_sem=t_send.at[0], recv_sem=t_recv.at[0],
+            device_id={"tm": inner}, device_id_type=MESH,
+        )
+
+    def swap():
+        return pltpu.make_async_remote_copy(
+            src_ref=term_ref, dst_ref=other_ref, send_sem=t_send.at[1], recv_sem=t_recv.at[1],
+            device_id={"tm": inner}, device_id_type=MESH,
+        )
+
+    def spread_out():
+        return pltpu.make_async_remote_copy(
+            src_ref=tot_ref, dst_ref=tot_ref, send_sem=t_send.at[2], recv_sem=t_recv.at[2],
+            device_id={"tm": outer}, device_id_type=MESH,
+        )
+
+    def inward():
+        @pl.when(place > 0)
+        def _():
+            gather().wait_recv()
+            term_ref[...] += part_ref[...]
+
+        @pl.when(place < half - 1)
+        def _():
+            gather().start()
+
+        @pl.when(place == half - 1)
+        def _():
+            swap().start()
+
+    def outward():
+        @pl.when(place == half - 1)
+        def _():
+            swap().wait_recv()
+            tot_ref[...] = term_ref[...] + other_ref[...]
+
+        @pl.when(place < half - 1)
+        def _():
+            spread_out().wait_recv()
+
+        @pl.when(place > 0)
+        def _():
+            spread_out().start()
+
+    def settle():
+        @pl.when(place < half - 1)
+        def _():
+            gather().wait_send()
+
+        @pl.when(place == half - 1)
+        def _():
+            swap().wait_send()
+
+        @pl.when(place > 0)
+        def _():
+            spread_out().wait_send()
+
     def relay(ref, base, number, c_ref, cs_ref, e_ref, want):
         def piece(chunk):
             return pl.ds(pl.multiple_of(chunk * TILE, TILE), TILE)
@@ -203,13 +280,6 @@
                 device_id={"tm": sooner}, device_id_type=MESH,
             )
 
-        def total(chunk):
-            return pltpu.make_async_remote_copy(
-                src_ref=tot_ref.at[piece(chunk)], dst_ref=tot_ref.at[piece(chunk)],
-                send_sem=t_send.at[chunk], recv_sem=t_recv.at[chunk],
-                device_id={"tm": sooner}, device_id_type=MESH,
-            )
-
         @pl.when(k == 0)
         def _():
             c_ref[...] = jnp.zeros(c_ref.shape, jnp.float32)
@@ -219,7 +289,13 @@
             for f in range(3):
                 e_ref[f] = ref[base + f, mine, :span]
 
+        turns = count + SKEW * (n - 1)
+
         def turn(i, nothing):
+            if want:
+                pl.when(i == 8 * place)(inward)
+                pl.when(i == jnp.minimum(8 * (n - 1 - place), turns - 1))(outward)
+
             ahead = i - SKEW * k
 
             @pl.when((ahead >= 0) & (ahead < count))
@@ -237,14 +313,7 @@
                         cs_ref[f, here, :] = ref[base + f, there, :span] + gain_ref[f, here, :] * (
                             c_ref[f, here, :] - old_ref[f, here, :]
                         )
-                    if want:
-                        cs_ref[3, here, :] = c_ref[3, here, :] + term_ref[here, :]
                     forward(ahead).start()
-
-                if want:
-                    @pl.when(k == n - 1)
-                    def _():
-                        tot_ref[here, :] = c_ref[3, here, :] + term_ref[here, :]
 
             behind = i - SKEW * (n - 1 - k)
 
@@ -258,22 +327,9 @@
                 def _():
                     back(behind).start()
 
-            if want:
-                final = behind - SKEW * (n - 1)
-
-                @pl.when((final >= 0) & (final < count))
-                def _():
-                    @pl.when(k < n - 1)
-                    def _():
-                        total(final).wait_recv()
-
-                    @pl.when(k > 0)
-                    def _():
-                        total(final).start()
-
             return nothing
 
-        lax.fori_loop(0, count + SKEW * (n - 1) * (2 if want else 1), turn, 0)
+        lax.fori_loop(0, turns, turn, 0)
 
         for f in range(3):
             power = e_ref[f]
@@ -294,8 +350,6 @@
             @pl.when(k > 0)
             def _():
                 back(chunk).wait_send()
-                if want:
-                    total(chunk).wait_send()
 
             return nothing
 
@@ -308,6 +362,7 @@
     exchange(y_ref, 1, (0.0,) * 3)
     sweep(y_ref, 0, True)
 
+    loads[7].wait()
     weight = 0.5 * x_ref[1, mine, :span] / x_ref[0, mine, :span]
     term = jnp.zeros((rows, span), jnp.float32)
     for f in range(4):
@@ -325,6 +380,7 @@
 
     finish_second = relay(y_ref, 0, 1, c2_ref, cs2_ref, e2_ref, True)
     grad_ref[...] = tot_ref[:, :cols] * (1.0 / (n * STEPS))
+    settle()
     finish_first()
     finish_second()
 
@@ -338,12 +394,12 @@
     wid = -(-(cols + 2 * WIDE) // LANES) * LANES
     span = -(-cols // LANES) * LANES
     count = rows // TILE
-    assert rows % TILE == 0 and rows >= WIDE and wid - LANES <= cols
+    assert n % 2 == 0 and rows % TILE == 0 and rows >= WIDE and wid - LANES <= cols
     counts = np.arange(1, n * STEPS + 1)
     angle = 2.0 * math.pi * counts / (n * STEPS)
     trig = jnp.asarray(np.stack([np.cos(angle), np.sin(angle)], axis=1).reshape(-1), jnp.float32)
     f32 = jnp.float32
-    vmem, smem = pl.BlockSpec(memory_space=pltpu.VMEM), pl.BlockSpec(memory_space=pltpu.SMEM)
+    vmem = pl.BlockSpec(memory_space=pltpu.VMEM)
     dma = pltpu.SemaphoreType.DMA
     return pl.pallas_call(
         functools.partial(kernel, sizes),
@@ -351,9 +407,18 @@
             jax.ShapeDtypeStruct((1, 3, rows, cols), f32),
             jax.ShapeDtypeStruct((rows, cols), f32),
         ),
-        in_specs=[vmem, vmem, smem, vmem, vmem, vmem, vmem, smem],
+        in_specs=[pl.BlockSpec(memory_space=pl.ANY)] * 8,
         out_specs=(vmem, vmem),
         scratch_shapes=[
+            pltpu.VMEM((rows, cols), jnp.int32),
+            pltpu.VMEM((rows, cols), jnp.int32),
+            pltpu.SMEM(depth_levels.shape, f32),
+            pltpu.VMEM((rows, cols), f32),
+            pltpu.VMEM(tide_force.shape, f32),
+            pltpu.VMEM(forward_flow.shape, f32),
+            pltpu.VMEM(guess.shape, f32),
+            pltpu.SMEM(trig.shape, f32),
+            dma((8,)),
             pltpu.VMEM((8, high, wid), f32),
             pltpu.VMEM((3, high, wid), f32),
             pltpu.VMEM((9, high, wid), f32),
@@ -368,16 +433,18 @@
             pltpu.VMEM((3, rows, span), f32),
             pltpu.VMEM((3, rows, span), f32),
             pltpu.VMEM((3, rows, span), f32),
-            pltpu.VMEM((4, rows, span), f32),
-            pltpu.VMEM((4, rows, span), f32),
-            pltpu.VMEM((3, rows, span), f32),
+            pltpu.VMEM((3, rows, span), f32),
+            pltpu.VMEM((3, rows, span), f32),
+            pltpu.VMEM((3, rows, span), f32),
+            pltpu.VMEM((rows, span), f32),
+            pltpu.VMEM((rows, span), f32),
             pltpu.VMEM((rows, span), f32),
             dma((4,)), dma((4,)), dma((4,)), dma((4,)),
             dma((2, count)), dma((2, count)), dma((2, count)), dma((2, count)),
-            dma((count,)), dma((count,)),
+            dma((3,)), dma((3,)),
         ],
         compiler_params=pltpu.CompilerParams(
-            collective_id=0, has_side_effects=True, vmem_limit_bytes=40 * 1024 * 1024
+            collective_id=0, has_side_effects=True, vmem_limit_bytes=56 * 1024 * 1024
         ),
         name="parareal",
     )(depth_class, ocean_mask, depth_levels, drag, tide_force, forward_flow, guess, trig)

time: 126 us -> 104 us (0.83)
  Pallas kernels: 117 us -> 101 us
  local copies, waits for them, and re-layouts: 8.84 us -> 2.67 us
    pallas_call x1, Pallas kernels: 117 us -> 101 us  [shards(): pl.pallas_call(functools.partial(kernel, sizes), out_shape=(jax.ShapeDtyp...]
    unnamed x18 -> x4, local copies, waits for them, and re-layouts: 8.84 us -> 2.67 us
where the time goes in v2:
time: 104 us
  Pallas kernels  101 us (97%)
  local copies, waits for them, and re-layouts  2.67 us (3%)
    pallas_call x1, Pallas kernels, shards(): pl.pallas_call(functools.partial(kernel, sizes), out_shape=(jax.ShapeDtyp...  101 us
    unnamed x4, local copies, waits for them, and re-layouts  2.67 us

profile of v2, /device:TPU:0, one launch (start us, length us, event | category | flops | bytes accessed | tf_op | source)
XLA Modules:
  0.0 104.3 jit_solution(8350121860274626110)
XLA Ops:
  0.6 101.0 %parareal.1 = (f32[1,3,136,384]{3,2,1,0:T(8,128)}, f32[136,384]{1,0:T(8,128)}) custom-call(s32[136,384]{1,0:T(8,128)} %cls_hbm.1, s32[136,384]{1,0:T(8,128)} %ocean_hbm.1, f32[32]{0:T(128)} %lev_hbm.1, f32[136,384]{1,0:T(8,128)} %drag_hbm.1, f32[2,136,384]{2,1,0:T(8,128)} %force_hbm.1, f32[4,136,384]{2,1,0:T(8,128)} %flow_hbm.1, ...), custom_call_target="tpu_custom_call" | custom-call | tf_op jit(solution)/shard_map/parareal/pallas_call | solution.py:404
  101.6 0.0 copy-start
  101.6 2.0 %copy.12 = f32[1,3,136,384]{3,2,1,0:T(8,128)} copy(f32[1,3,136,384]{3,2,1,0:T(8,128)} %get-tuple-element.4) | data formatting | bytes 1253376
  103.6 0.0 copy-done
  103.6 0.7 copy.13
Async XLA Ops:
  101.6 2.0 %copy-start = (f32[136,384]{1,0:T(8,128)S(1)}, f32[136,384]{1,0:T(8,128)}, u32[]{:S(2)}) copy-start(f32[136,384]{1,0:T(8,128)} %get-tuple-element.5) | copy-start | bytes 626692

commit v3 on v2

--- a/solution.py
+++ b/solution.py
@@ -15,7 +15,7 @@
 WIDE = STEPS
 LANES = 128
 TILE = 8
-SKEW = 4
+SKEW = 5
 
 MESH = pl.DeviceIdType.MESH
 
@@ -54,6 +54,9 @@
         ("lat", north), ("lat", south), ("lon", east), ("lon", west), ("tm", later), ("tm", sooner)
     ):
         pl.semaphore_signal(barrier, inc=1, device_id={axis: spot}, device_id_type=MESH)
+    for y in (north, south):
+        for x in (east, west):
+            pl.semaphore_signal(barrier, inc=1, device_id={"lat": y, "lon": x}, device_id_type=MESH)
 
     mine = pl.ds(WIDE, rows)
     loads[0].wait()
@@ -73,7 +76,7 @@
         x_ref[3 + f, mine, :cols] = force_ref[f]
     for f in range(3):
         x_ref[5 + f, mine, :cols] = guess_ref[0, f]
-    pl.semaphore_wait(barrier, 6)
+    pl.semaphore_wait(barrier, 10)
 
     def exchange(ref, number, fills):
         fields = len(fills)
@@ -91,33 +94,37 @@
         )
         up.start()
         down.start()
-        up.wait()
-        down.wait()
-        lane = lax.broadcasted_iota(jnp.int32, (high, LANES), 1)
+        small = lax.broadcasted_iota(jnp.int32, (rows, LANES), 1)
         last = (cols - WIDE) // LANES * LANES
         inset = cols - WIDE - last
         eastern = western = None
         for f in range(fields):
-            e = pltpu.roll(ref[f, :, last : last + LANES], (WIDE * f - inset) % LANES, 1)
-            w = pltpu.roll(ref[f, :, :LANES], WIDE * f, 1) if f else ref[f, :, :LANES]
-            eastern = jnp.where(lane >= WIDE * f, e, eastern) if f else e
-            western = jnp.where(lane >= WIDE * f, w, western) if f else w
+            e = pltpu.roll(ref[f, mine, last : last + LANES], (WIDE * f - inset) % LANES, 1)
+            w = ref[f, mine, :LANES]
+            w = pltpu.roll(w, WIDE * f, 1) if f else w
+            eastern = jnp.where(small >= WIDE * f, e, eastern) if f else e
+            western = jnp.where(small >= WIDE * f, w, western) if f else w
         east_out[number] = eastern
         west_out[number] = western
-        right = pltpu.make_async_remote_copy(
-            src_ref=east_out.at[number], dst_ref=west_in.at[number],
-            send_sem=col_send.at[2 * number], recv_sem=col_recv.at[2 * number],
-            device_id={"lon": east}, device_id_type=MESH,
-        )
-        left = pltpu.make_async_remote_copy(
-            src_ref=west_out.at[number], dst_ref=east_in.at[number],
-            send_sem=col_send.at[2 * number + 1], recv_sem=col_recv.at[2 * number + 1],
-            device_id={"lon": west}, device_id_type=MESH,
-        )
-        right.start()
-        left.start()
-        right.wait()
-        left.wait()
+        copies = [up, down]
+        for side, (x, source, target) in enumerate(((east, east_out, west_in), (west, west_out, east_in))):
+            for y, first, extent, landing in (
+                (None, 0, rows, WIDE), (north, rows - WIDE, WIDE, 0), (south, 0, WIDE, WIDE + rows)
+            ):
+                slot = 6 * number + len(copies) - 2
+                copies.append(
+                    pltpu.make_async_remote_copy(
+                        src_ref=source.at[number, pl.ds(first, extent)],
+                        dst_ref=target.at[number, pl.ds(landing, extent)],
+                        send_sem=col_send.at[slot], recv_sem=col_recv.at[slot],
+                        device_id={"lon": x} if y is None else {"lat": y, "lon": x},
+                        device_id_type=MESH,
+                    )
+                )
+                copies[-1].start()
+        for copy in copies:
+            copy.wait()
+        lane = lax.broadcasted_iota(jnp.int32, (high, LANES), 1)
         start = wid - LANES
         own = cols - start
         from_east, from_west = east_in[number], west_in[number]
@@ -426,8 +433,8 @@
             pltpu.VMEM((3, rows, span), f32),
             pltpu.VMEM((3, rows, span), f32),
             pltpu.VMEM((rows, span), f32),
-            pltpu.VMEM((2, high, LANES), f32),
-            pltpu.VMEM((2, high, LANES), f32),
+            pltpu.VMEM((2, rows, LANES), f32),
+            pltpu.VMEM((2, rows, LANES), f32),
             pltpu.VMEM((2, high, LANES), f32),
             pltpu.VMEM((2, high, LANES), f32),
             pltpu.VMEM((3, rows, span), f32),
@@ -439,7 +446,7 @@
             pltpu.VMEM((rows, span), f32),
             pltpu.VMEM((rows, span), f32),
             pltpu.VMEM((rows, span), f32),
-            dma((4,)), dma((4,)), dma((4,)), dma((4,)),
+            dma((4,)), dma((4,)), dma((12,)), dma((12,)),
             dma((2, count)), dma((2, count)), dma((2, count)), dma((2, count)),
             dma((3,)), dma((3,)),
         ],

time: 104 us -> 96.8 us (0.931)
  Pallas kernels: 101 us -> 93.3 us
    pallas_call x1, Pallas kernels: 101 us -> 93.3 us  [shards(): pl.pallas_call(functools.partial(kernel, sizes), out_shape=(jax.ShapeDtyp...]
where the time goes in v3:
time: 96.8 us; the launch traced here: 96.7 us
  Pallas kernels  93.3 us (96%)
  local copies, waits for them, and re-layouts  2.67 us (3%)
    pallas_call x1, Pallas kernels, shards(): pl.pallas_call(functools.partial(kernel, sizes), out_shape=(jax.ShapeDtyp...  93.3 us
    unnamed x4, local copies, waits for them, and re-layouts  2.67 us

profile of v3, /device:TPU:0, one launch (start us, length us, event | category | flops | bytes accessed | tf_op | source)
XLA Modules:
  0.0 96.7 jit_solution(3707273859509477785)
XLA Ops:
  0.6 93.3 %parareal.1 = (f32[1,3,136,384]{3,2,1,0:T(8,128)}, f32[136,384]{1,0:T(8,128)}) custom-call(s32[136,384]{1,0:T(8,128)} %cls_hbm.1, s32[136,384]{1,0:T(8,128)} %ocean_hbm.1, f32[32]{0:T(128)} %lev_hbm.1, f32[136,384]{1,0:T(8,128)} %drag_hbm.1, f32[2,136,384]{2,1,0:T(8,128)} %force_hbm.1, f32[4,136,384]{2,1,0:T(8,128)} %flow_hbm.1, ...), custom_call_target="tpu_custom_call" | custom-call | tf_op jit(solution)/shard_map/parareal/pallas_call | solution.py:411
  94.0 0.0 copy-start
  94.0 2.0 %copy.12 = f32[1,3,136,384]{3,2,1,0:T(8,128)} copy(f32[1,3,136,384]{3,2,1,0:T(8,128)} %get-tuple-element.4) | data formatting | bytes 1253376
  96.0 0.0 copy-done
  96.0 0.7 copy.13
Async XLA Ops:
  94.0 2.0 %copy-start = (f32[136,384]{1,0:T(8,128)S(1)}, f32[136,384]{1,0:T(8,128)}, u32[]{:S(2)}) copy-start(f32[136,384]{1,0:T(8,128)} %get-tuple-element.5) | copy-start | bytes 626692

commit v4 on v3

--- a/solution.py
+++ b/solution.py
@@ -15,6 +15,7 @@
 WIDE = STEPS
 LANES = 128
 TILE = 8
+EARLY = 8
 SKEW = 5
 
 MESH = pl.DeviceIdType.MESH
@@ -24,7 +25,7 @@
     sizes, cls_hbm, ocean_hbm, lev_hbm, drag_hbm, force_hbm, flow_hbm, guess_hbm, trig_hbm,
     out_ref, grad_ref,
     cls_ref, ocean_ref, lev_ref, drag_ref, force_ref, flow_ref, guess_ref, trig_ref, load_sem,
-    x_ref, y_ref, st_ref, acc_ref, gain_ref, old_ref, term_ref, east_out, west_out, east_in, west_in,
+    x_ref, y_ref, b_ref, end_ref, st_ref, acc_ref, gain_ref, old_ref, term_ref, east_out, west_out, east_in, west_in,
     c1_ref, cs1_ref, e1_ref, c2_ref, cs2_ref, e2_ref, part_ref, other_ref, tot_ref,
     row_send, row_recv, col_send, col_recv,
     c_send, c_recv, e_send, e_recv, t_send, t_recv,
@@ -33,7 +34,8 @@
     rows, cols = ocean_ref.shape
     high, wid = x_ref.shape[1], x_ref.shape[2]
     span = c1_ref.shape[2]
-    block = TILE * max(d for d in (1, 2, 3) if (high // TILE) % d == 0)
+    block = 2 * TILE
+    cut = EARLY * TILE
     count = rows // TILE
     k, lat, lon = lax.axis_index("tm"), lax.axis_index("lat"), lax.axis_index("lon")
     north, south = lax.rem(lat + 1, n_lat), lax.rem(lat + n_lat - 1, n_lat)
@@ -138,16 +140,17 @@
 
     exchange(x_ref, 0, (1.0,) + (0.0,) * 7)
 
-    def below(ref, f, r):
+    def below(ref, f, r, extent):
         if r == 0:
-            return pltpu.roll(ref[f, :block, :], 1, 0)
-        return pltpu.roll(ref[f, r - TILE : r + block, :], 1, 0)[TILE:]
+            return pltpu.roll(ref[f, :extent, :], 1, 0)
+        return pltpu.roll(ref[f, r - TILE : r + extent, :], 1, 0)[TILE:]
 
     for r in range(0, high, block):
-        here = pl.ds(r, block)
+        tall = min(block, high - r)
+        here = pl.ds(r, tall)
         d, m, g = x_ref[0, here, :], x_ref[1, here, :], x_ref[2, here, :]
         for side, shifted in enumerate(
-            (lambda f, v: pltpu.roll(v, 1, 1), lambda f, v: below(x_ref, f, r))
+            (lambda f, v: pltpu.roll(v, 1, 1), lambda f, v: below(x_ref, f, r, tall))
         ):
             both = d + shifted(0, d)
             wet = m * shifted(1, m)
@@ -165,46 +168,74 @@
         gain_ref[1 + side] = g
     acc_ref[...] = jnp.zeros(acc_ref.shape, jnp.float32)
 
-    def sweep(ref, base, want):
-        def step(t, nothing):
-            cosine = trig_ref[2 * (k * STEPS + t)]
-            sine = trig_ref[2 * (k * STEPS + t) + 1]
-            carry = None
-            for r in reversed(range(0, high, block)):
-                here = pl.ds(r, block)
-                a = ref[base, here, :]
-                p = st_ref[0, here, :] * ref[base + 1, here, :] - st_ref[2, here, :] * (
-                    a - pltpu.roll(a, 1, 1)
-                )
-                q = st_ref[1, here, :] * ref[base + 2, here, :] - st_ref[3, here, :] * (
-                    a - below(ref, base, r)
-                )
-                u = st_ref[4, here, :] * p
-                v = st_ref[5, here, :] * q
-                if carry is None:
-                    v_north = pltpu.roll(v, block - 1, 0)
-                else:
-                    v_north = pltpu.roll(
-                        jnp.concatenate([v, carry], axis=0), block + TILE - 1, 0
-                    )[:block]
-                carry = v[:TILE]
-                spread = (pltpu.roll(u, wid - 1, 1) - u) + (v_north - v)
-                ref[base, here, :] = st_ref[6, here, :] * (a - spread) + (
-                    st_ref[7, here, :] * cosine + st_ref[8, here, :] * sine
-                )
-                ref[base + 1, here, :] = p
-                ref[base + 2, here, :] = q
-                if want:
-                    low, top = max(r, WIDE), min(r + block, WIDE + rows + TILE)
-                    part = pl.ds(low, top - low)
-                    p, q = p[low - r : top - r], q[low - r : top - r]
-                    acc_ref[0, part, :] += cosine * p
-                    acc_ref[1, part, :] += sine * p
-                    acc_ref[2, part, :] += cosine * q
-                    acc_ref[3, part, :] += sine * q
+    def advance(ref, base, offset, extent, first, end, want, t):
+        cosine = trig_ref[2 * (k * STEPS + t)]
+        sine = trig_ref[2 * (k * STEPS + t) + 1]
+        carry = None
+        for r in reversed(range(0, extent, block)):
+            tall = min(block, extent - r)
+            here, there = pl.ds(r, tall), pl.ds(offset + r, tall)
+            a = ref[base, here, :]
+            p = st_ref[0, there, :] * ref[base + 1, here, :] - st_ref[2, there, :] * (
+                a - pltpu.roll(a, 1, 1)
+            )
+            q = st_ref[1, there, :] * ref[base + 2, here, :] - st_ref[3, there, :] * (
+                a - below(ref, base, r, tall)
+            )
+            u = st_ref[4, there, :] * p
+            v = st_ref[5, there, :] * q
+            if carry is None:
+                v_north = pltpu.roll(v, tall - 1, 0)
+            else:
+                v_north = pltpu.roll(
+                    jnp.concatenate([v, carry], axis=0), tall + TILE - 1, 0
+                )[:tall]
+            carry = v[:TILE]
+            spread = (pltpu.roll(u, wid - 1, 1) - u) + (v_north - v)
+            ref[base, here, :] = st_ref[6, there, :] * (a - spread) + (
+                st_ref[7, there, :] * cosine + st_ref[8, there, :] * sine
+            )
+            ref[base + 1, here, :] = p
+            ref[base + 2, here, :] = q
+            low, top = max(r, first), min(r + tall, end)
+            if want and low < top:
+                part = pl.ds(offset + low, top - low)
+                p, q = p[low - r : top - r], q[low - r : top - r]
+                acc_ref[0, part, :] += cosine * p
+                acc_ref[1, part, :] += sine * p
+                acc_ref[2, part, :] += cosine * q
+                acc_ref[3, part, :] += sine * q
+
+    def sweep(ref, base, want, turn, e_ref):
+        def keep(source, start, first, extent):
+            for f in range(3):
+                end_ref[f, pl.ds(first, extent), :] = source[start + f, pl.ds(WIDE, extent), :span]
+
+            @pl.when(k == n - 1)
+            def _():
+                for f in range(3):
+                    e_ref[f, pl.ds(first, extent), :] = source[start + f, pl.ds(WIDE, extent), :span]
+
+        for f in range(3):
+            b_ref[f] = ref[base + f, cut:, :]
+
+        def lower(t, nothing):
+            advance(ref, base, 0, cut + 2 * WIDE, WIDE, WIDE + cut, want, t)
             return nothing
 
-        lax.fori_loop(0, STEPS, step, 0)
+        lax.fori_loop(0, STEPS, lower, 0)
+        keep(ref, base, 0, cut)
+
+        def upper(i, nothing):
+            def one(t, nothing):
+                advance(b_ref, 0, cut, high - cut, WIDE, WIDE + rows - cut + TILE, want, t)
+                return nothing
+
+            lax.fori_loop(i * (STEPS // EARLY), (i + 1) * (STEPS // EARLY), one, 0)
+            return turn(i, nothing)
+
+        lax.fori_loop(0, EARLY, upper, 0)
+        keep(b_ref, 0, cut, rows - cut)
 
     half = n // 2
     place = jnp.where(k < half, k, n - 1 - k)
@@ -269,7 +300,7 @@
         def _():
             spread_out().wait_send()
 
-    def relay(ref, base, number, c_ref, cs_ref, e_ref, want):
+    def relay(number, c_ref, cs_ref, e_ref, want):
         def piece(chunk):
             return pl.ds(pl.multiple_of(chunk * TILE, TILE), TILE)
 
@@ -291,17 +322,12 @@
         def _():
             c_ref[...] = jnp.zeros(c_ref.shape, jnp.float32)
 
-        @pl.when(k == n - 1)
-        def _():
-            for f in range(3):
-                e_ref[f] = ref[base + f, mine, :span]
-
         turns = count + SKEW * (n - 1)
 
         def turn(i, nothing):
             if want:
-                pl.when(i == 8 * place)(inward)
-                pl.when(i == jnp.minimum(8 * (n - 1 - place), turns - 1))(outward)
+                pl.when(i == EARLY + 8 * place)(inward)
+                pl.when(i == jnp.minimum(EARLY + 8 * (n - 1 - place), turns - 1))(outward)
 
             ahead = i - SKEW * k
 
@@ -312,12 +338,11 @@
                     forward(ahead).wait_recv()
 
                 here = piece(ahead)
-                there = pl.ds(pl.multiple_of(WIDE + ahead * TILE, TILE), TILE)
 
                 @pl.when(k < n - 1)
                 def _():
                     for f in range(3):
-                        cs_ref[f, here, :] = ref[base + f, there, :span] + gain_ref[f, here, :] * (
+                        cs_ref[f, here, :] = end_ref[f, here, :] + gain_ref[f, here, :] * (
                             c_ref[f, here, :] - old_ref[f, here, :]
                         )
                     forward(ahead).start()
@@ -336,18 +361,19 @@
 
             return nothing
 
-        lax.fori_loop(0, turns, turn, 0)
-
-        for f in range(3):
-            power = e_ref[f]
-            for j in range(n - 1):
-                power = power * jnp.where(j < k, gain_ref[f], 1.0)
-            fresh = c_ref[f] + power
-            if want:
-                out_ref[0, f] = fresh[:, :cols]
-            else:
-                old_ref[f] = fresh
-                y_ref[f, mine, :span] = fresh
+        def close():
+            lax.fori_loop(EARLY, turns, turn, 0)
+
+            for f in range(3):
+                power = e_ref[f]
+                for j in range(n - 1):
+                    power = power * jnp.where(j < k, gain_ref[f], 1.0)
+                fresh = c_ref[f] + power
+                if want:
+                    out_ref[0, f] = fresh[:, :cols]
+                else:
+                    old_ref[f] = fresh
+                    y_ref[f, mine, :span] = fresh
 
         def sent(chunk, nothing):
             @pl.when(k < n - 1)
@@ -360,14 +386,16 @@
 
             return nothing
 
-        return lambda: lax.fori_loop(0, count, sent, 0)
+        return turn, close, lambda: lax.fori_loop(0, count, sent, 0)
 
     for f in range(3):
         old_ref[f] = x_ref[5 + f, mine, :span]
-    sweep(x_ref, 5, False)
-    finish_first = relay(x_ref, 5, 0, c1_ref, cs1_ref, e1_ref, False)
+    turn, close, finish_first = relay(0, c1_ref, cs1_ref, e1_ref, False)
+    sweep(x_ref, 5, False, turn, e1_ref)
+    close()
     exchange(y_ref, 1, (0.0,) * 3)
-    sweep(y_ref, 0, True)
+    turn, close, finish_second = relay(1, c2_ref, cs2_ref, e2_ref, True)
+    sweep(y_ref, 0, True, turn, e2_ref)
 
     loads[7].wait()
     weight = 0.5 * x_ref[1, mine, :span] / x_ref[0, mine, :span]
@@ -385,7 +413,7 @@
         term = term + flow * mid
     term_ref[...] = weight * term
 
-    finish_second = relay(y_ref, 0, 1, c2_ref, cs2_ref, e2_ref, True)
+    close()
     grad_ref[...] = tot_ref[:, :cols] * (1.0 / (n * STEPS))
     settle()
     finish_first()
@@ -401,7 +429,7 @@
     wid = -(-(cols + 2 * WIDE) // LANES) * LANES
     span = -(-cols // LANES) * LANES
     count = rows // TILE
-    assert n % 2 == 0 and rows % TILE == 0 and rows >= WIDE and wid - LANES <= cols
+    assert n % 2 == 0 and count > EARLY and rows % TILE == 0 and rows >= WIDE and wid - LANES <= cols
     counts = np.arange(1, n * STEPS + 1)
     angle = 2.0 * math.pi * counts / (n * STEPS)
     trig = jnp.asarray(np.stack([np.cos(angle), np.sin(angle)], axis=1).reshape(-1), jnp.float32)
@@ -428,6 +456,8 @@
             dma((8,)),
             pltpu.VMEM((8, high, wid), f32),
             pltpu.VMEM((3, high, wid), f32),
+            pltpu.VMEM((3, high - EARLY * TILE, wid), f32),
+            pltpu.VMEM((3, rows, span), f32),
             pltpu.VMEM((9, high, wid), f32),
             pltpu.VMEM((4, high, wid), f32),
             pltpu.VMEM((3, rows, span), f32),

time: 96.8 us -> 90.7 us (0.937)
  Pallas kernels: 93.3 us -> 87.3 us
    pallas_call x1, Pallas kernels: 93.3 us -> 87.3 us  [shards(): pl.pallas_call(functools.partial(kernel, sizes), out_shape=(jax.ShapeDtyp...]
where the time goes in v4:
time: 90.7 us; the launch traced here: 90.6 us
  Pallas kernels  87.3 us (96%)
  local copies, waits for them, and re-layouts  2.67 us (3%)
    pallas_call x1, Pallas kernels, shards(): pl.pallas_call(functools.partial(kernel, sizes), out_shape=(jax.ShapeDtyp...  87.3 us
    unnamed x4, local copies, waits for them, and re-layouts  2.67 us

profile of v4, /device:TPU:0, one launch (start us, length us, event | category | flops | bytes accessed | tf_op | source)
XLA Modules:
  0.0 90.6 jit_solution(3522037455776655687)
XLA Ops:
  0.6 87.3 %parareal.1 = (f32[1,3,136,384]{3,2,1,0:T(8,128)}, f32[136,384]{1,0:T(8,128)}) custom-call(s32[136,384]{1,0:T(8,128)} %cls_hbm.1, s32[136,384]{1,0:T(8,128)} %ocean_hbm.1, f32[32]{0:T(128)} %lev_hbm.1, f32[136,384]{1,0:T(8,128)} %drag_hbm.1, f32[2,136,384]{2,1,0:T(8,128)} %force_hbm.1, f32[4,136,384]{2,1,0:T(8,128)} %flow_hbm.1, ...), custom_call_target="tpu_custom_call" | custom-call | tf_op jit(solution)/shard_map/parareal/pallas_call | solution.py:439
  87.9 0.0 copy-start
  87.9 2.0 %copy.12 = f32[1,3,136,384]{3,2,1,0:T(8,128)} copy(f32[1,3,136,384]{3,2,1,0:T(8,128)} %get-tuple-element.4) | data formatting | bytes 1253376
  89.9 0.0 copy-done
  89.9 0.7 copy.13
Async XLA Ops:
  87.9 2.0 %copy-start = (f32[136,384]{1,0:T(8,128)S(1)}, f32[136,384]{1,0:T(8,128)}, u32[]{:S(2)}) copy-start(f32[136,384]{1,0:T(8,128)} %get-tuple-element.5) | copy-start | bytes 626692

commit v5 on v4

--- a/solution.py
+++ b/solution.py
@@ -36,6 +36,7 @@
     span = c1_ref.shape[2]
     block = 2 * TILE
     cut = EARLY * TILE
+    mid = cut + 2 * WIDE
     count = rows // TILE
     k, lat, lon = lax.axis_index("tm"), lax.axis_index("lat"), lax.axis_index("lon")
     north, south = lax.rem(lat + 1, n_lat), lax.rem(lat + n_lat - 1, n_lat)
@@ -78,24 +79,27 @@
         x_ref[3 + f, mine, :cols] = force_ref[f]
     for f in range(3):
         x_ref[5 + f, mine, :cols] = guess_ref[0, f]
+        old_ref[f] = x_ref[5 + f, mine, :span]
     pl.semaphore_wait(barrier, 10)
 
-    def exchange(ref, number, fills):
+    def exchange(ref, number, fills, moves):
         fields = len(fills)
-        up = pltpu.make_async_remote_copy(
-            src_ref=ref.at[:, pl.ds(rows, WIDE), pl.ds(0, span)],
-            dst_ref=ref.at[:, pl.ds(0, WIDE), pl.ds(0, span)],
-            send_sem=row_send.at[2 * number], recv_sem=row_recv.at[2 * number],
-            device_id={"lat": north}, device_id_type=MESH,
-        )
-        down = pltpu.make_async_remote_copy(
-            src_ref=ref.at[:, pl.ds(WIDE, WIDE), pl.ds(0, span)],
-            dst_ref=ref.at[:, pl.ds(WIDE + rows, WIDE), pl.ds(0, span)],
-            send_sem=row_send.at[2 * number + 1], recv_sem=row_recv.at[2 * number + 1],
-            device_id={"lat": south}, device_id_type=MESH,
-        )
-        up.start()
-        down.start()
+        low, tops = [], []
+        for source, start, skip, landing, extent in moves:
+            for copies, y, first, last in (
+                (low, north, rows - WIDE, 0), (tops, south, 0, WIDE + rows)
+            ):
+                slot = 4 * number + len(low) + len(tops)
+                copies.append(
+                    pltpu.make_async_remote_copy(
+                        src_ref=source.at[pl.ds(start, extent), pl.ds(skip + first, WIDE), pl.ds(0, span)],
+                        dst_ref=ref.at[pl.ds(landing, extent), pl.ds(last, WIDE), pl.ds(0, span)],
+                        send_sem=row_send.at[slot], recv_sem=row_recv.at[slot],
+                        device_id={"lat": y}, device_id_type=MESH,
+                    )
+                )
+        for copy in low:
+            copy.start()
         small = lax.broadcasted_iota(jnp.int32, (rows, LANES), 1)
         last = (cols - WIDE) // LANES * LANES
         inset = cols - WIDE - last
@@ -108,12 +112,12 @@
             western = jnp.where(small >= WIDE * f, w, western) if f else w
         east_out[number] = eastern
         west_out[number] = western
-        copies = [up, down]
-        for side, (x, source, target) in enumerate(((east, east_out, west_in), (west, west_out, east_in))):
-            for y, first, extent, landing in (
-                (None, 0, rows, WIDE), (north, rows - WIDE, WIDE, 0), (south, 0, WIDE, WIDE + rows)
+        slot = 8 * number
+        for x, source, target in ((east, east_out, west_in), (west, west_out, east_in)):
+            for copies, y, first, extent, landing in (
+                (low, None, 0, mid - WIDE, WIDE), (low, north, rows - WIDE, WIDE, 0),
+                (tops, None, mid - WIDE, rows + WIDE - mid, mid), (tops, south, 0, WIDE, WIDE + rows),
             ):
-                slot = 6 * number + len(copies) - 2
                 copies.append(
                     pltpu.make_async_remote_copy(
                         src_ref=source.at[number, pl.ds(first, extent)],
@@ -123,57 +127,74 @@
                         device_id_type=MESH,
                     )
                 )
-                copies[-1].start()
-        for copy in copies:
-            copy.wait()
-        lane = lax.broadcasted_iota(jnp.int32, (high, LANES), 1)
-        start = wid - LANES
-        own = cols - start
-        from_east, from_west = east_in[number], west_in[number]
-        for f, fill in enumerate(fills):
-            e = pltpu.roll(from_east, (own - WIDE * f) % LANES, 1)
-            w = pltpu.roll(from_west, (LANES - WIDE - WIDE * f) % LANES, 1)
-            halo = jnp.where(lane < own + WIDE, e, jnp.where(lane >= LANES - WIDE, w, fill))
-            if own:
-                halo = jnp.where(lane < own, ref[f, :, start:], halo)
-            ref[f, :, start:] = halo
-
-    exchange(x_ref, 0, (1.0,) + (0.0,) * 7)
+                slot += 1
+        for copy in low[len(moves):] + tops:
+            copy.start()
+
+        def settle(copies, first, extent):
+            for copy in copies:
+                copy.wait()
+            lane = lax.broadcasted_iota(jnp.int32, (extent, LANES), 1)
+            start = wid - LANES
+            own = cols - start
+            here = pl.ds(first, extent)
+            from_east, from_west = east_in[number, here], west_in[number, here]
+            for f, fill in enumerate(fills):
+                e = pltpu.roll(from_east, (own - WIDE * f) % LANES, 1)
+                w = pltpu.roll(from_west, (LANES - WIDE - WIDE * f) % LANES, 1)
+                halo = jnp.where(lane < own + WIDE, e, jnp.where(lane >= LANES - WIDE, w, fill))
+                if own:
+                    halo = jnp.where(lane < own, ref[f, here, start:], halo)
+                ref[f, here, start:] = halo
+
+        settle(low, 0, mid)
+        return lambda: settle(tops, mid, high - mid)
+
+    rest = exchange(
+        x_ref, 0, (1.0,) + (0.0,) * 7, ((x_ref, 0, WIDE, 0, 5), (old_ref, 0, 0, 5, 3))
+    )
 
     def below(ref, f, r, extent):
         if r == 0:
             return pltpu.roll(ref[f, :extent, :], 1, 0)
         return pltpu.roll(ref[f, r - TILE : r + extent, :], 1, 0)[TILE:]
 
-    for r in range(0, high, block):
-        tall = min(block, high - r)
-        here = pl.ds(r, tall)
-        d, m, g = x_ref[0, here, :], x_ref[1, here, :], x_ref[2, here, :]
-        for side, shifted in enumerate(
-            (lambda f, v: pltpu.roll(v, 1, 1), lambda f, v: below(x_ref, f, r, tall))
-        ):
-            both = d + shifted(0, d)
-            wet = m * shifted(1, m)
-            st_ref[side, here, :] = wet * (1.0 - (g + shifted(2, g)) / both)
-            st_ref[2 + side, here, :] = 0.7 * wet
-            st_ref[4 + side, here, :] = 0.3 * both
-        st_ref[6, here, :] = m
-        st_ref[7, here, :] = m * x_ref[3, here, :]
-        st_ref[8, here, :] = m * x_ref[4, here, :]
-    gain_ref[0] = x_ref[1, mine, :span]
-    for side in range(2):
-        g = st_ref[side, mine, :span]
-        for _ in range(STEPS.bit_length() - 1):
-            g = g * g
-        gain_ref[1 + side] = g
+    def faces(first, last):
+        for r in range(first, last, block):
+            tall = min(block, last - r)
+            here = pl.ds(r, tall)
+            d, m, g = x_ref[0, here, :], x_ref[1, here, :], x_ref[2, here, :]
+            for side, shifted in enumerate(
+                (lambda f, v: pltpu.roll(v, 1, 1), lambda f, v: below(x_ref, f, r, tall))
+            ):
+                both = d + shifted(0, d)
+                wet = m * shifted(1, m)
+                st_ref[side, here, :] = wet * (1.0 - (g + shifted(2, g)) / both)
+                st_ref[2 + side, here, :] = 0.7 * wet
+                st_ref[4 + side, here, :] = 0.3 * both
+            st_ref[6, here, :] = m
+            st_ref[7, here, :] = m * x_ref[3, here, :]
+            st_ref[8, here, :] = m * x_ref[4, here, :]
+
+    def complete():
+        rest()
+        faces(mid, high)
+        gain_ref[0] = x_ref[1, mine, :span]
+        for side in range(2):
+            g = st_ref[side, mine, :span]
+            for _ in range(STEPS.bit_length() - 1):
+                g = g * g
+            gain_ref[1 + side] = g
+
+    faces(0, mid)
     acc_ref[...] = jnp.zeros(acc_ref.shape, jnp.float32)
 
-    def advance(ref, base, offset, extent, first, end, want, t):
+    def advance(ref, base, offset, start, stop, first, end, want, t):
         cosine = trig_ref[2 * (k * STEPS + t)]
         sine = trig_ref[2 * (k * STEPS + t) + 1]
         carry = None
-        for r in reversed(range(0, extent, block)):
-            tall = min(block, extent - r)
+        for r in reversed(range(start, stop, block)):
+            tall = min(block, stop - r)
             here, there = pl.ds(r, tall), pl.ds(offset + r, tall)
             a = ref[base, here, :]
             p = st_ref[0, there, :] * ref[base + 1, here, :] - st_ref[2, there, :] * (
@@ -206,7 +227,7 @@
                 acc_ref[2, part, :] += cosine * q
                 acc_ref[3, part, :] += sine * q
 
-    def sweep(ref, base, want, turn, e_ref):
+    def sweep(ref, base, want, turn, e_ref, between):
         def keep(source, start, first, extent):
             for f in range(3):
                 end_ref[f, pl.ds(first, extent), :] = source[start + f, pl.ds(WIDE, extent), :span]
@@ -217,24 +238,33 @@
                     e_ref[f, pl.ds(first, extent), :] = source[start + f, pl.ds(WIDE, extent), :span]
 
         for f in range(3):
-            b_ref[f] = ref[base + f, cut:, :]
-
-        def lower(t, nothing):
-            advance(ref, base, 0, cut + 2 * WIDE, WIDE, WIDE + cut, want, t)
-            return nothing
-
-        lax.fori_loop(0, STEPS, lower, 0)
+            b_ref[f, : mid - cut] = ref[base + f, cut:mid, :]
+
+        for trim in (0, TILE):
+            def lower(t, nothing):
+                advance(ref, base, 0, trim, mid - trim, WIDE, WIDE + cut, want, t)
+                return nothing
+
+            begin = STEPS // 2 if trim else 0
+            lax.fori_loop(begin, begin + STEPS // 2, lower, 0)
         keep(ref, base, 0, cut)
-
-        def upper(i, nothing):
-            def one(t, nothing):
-                advance(b_ref, 0, cut, high - cut, WIDE, WIDE + rows - cut + TILE, want, t)
-                return nothing
-
-            lax.fori_loop(i * (STEPS // EARLY), (i + 1) * (STEPS // EARLY), one, 0)
-            return turn(i, nothing)
-
-        lax.fori_loop(0, EARLY, upper, 0)
+        between()
+        for f in range(3):
+            b_ref[f, mid - cut :] = ref[base + f, mid:, :]
+
+        for trim in (0, TILE):
+            def upper(i, nothing):
+                def one(t, nothing):
+                    advance(
+                        b_ref, 0, cut, trim, high - cut - trim, WIDE, WIDE + rows - cut + TILE, want, t
+                    )
+                    return nothing
+
+                lax.fori_loop(i * (STEPS // EARLY), (i + 1) * (STEPS // EARLY), one, 0)
+                return turn(i, nothing)
+
+            begin = EARLY // 2 if trim else 0
+            lax.fori_loop(begin, begin + EARLY // 2, upper, 0)
         keep(b_ref, 0, cut, rows - cut)
 
     half = n // 2
@@ -388,14 +418,12 @@
 
         return turn, close, lambda: lax.fori_loop(0, count, sent, 0)
 
-    for f in range(3):
-        old_ref[f] = x_ref[5 + f, mine, :span]
     turn, close, finish_first = relay(0, c1_ref, cs1_ref, e1_ref, False)
-    sweep(x_ref, 5, False, turn, e1_ref)
+    sweep(x_ref, 5, False, turn, e1_ref, complete)
     close()
-    exchange(y_ref, 1, (0.0,) * 3)
+    rest_second = exchange(y_ref, 1, (0.0,) * 3, ((old_ref, 0, 0, 0, 3),))
     turn, close, finish_second = relay(1, c2_ref, cs2_ref, e2_ref, True)
-    sweep(y_ref, 0, True, turn, e2_ref)
+    sweep(y_ref, 0, True, turn, e2_ref, rest_second)
 
     loads[7].wait()
     weight = 0.5 * x_ref[1, mine, :span] / x_ref[0, mine, :span]
@@ -476,7 +504,7 @@
             pltpu.VMEM((rows, span), f32),
             pltpu.VMEM((rows, span), f32),
             pltpu.VMEM((rows, span), f32),
-            dma((4,)), dma((4,)), dma((12,)), dma((12,)),
+            dma((8,)), dma((8,)), dma((16,)), dma((16,)),
             dma((2, count)), dma((2, count)), dma((2, count)), dma((2, count)),
             dma((3,)), dma((3,)),
         ],

time: 90.7 us -> 87.5 us (0.965)
  Pallas kernels: 87.3 us -> 84 us
    pallas_call x1, Pallas kernels: 87.3 us -> 84 us  [shards(): pl.pallas_call(functools.partial(kernel, sizes), out_shape=(jax.ShapeDtyp...]
where the time goes in v5:
time: 87.5 us; the launch traced here: 87.3 us
  Pallas kernels  84 us (96%)
  local copies, waits for them, and re-layouts  2.67 us (3%)
    pallas_call x1, Pallas kernels, shards(): pl.pallas_call(functools.partial(kernel, sizes), out_shape=(jax.ShapeDtyp...  84 us
    unnamed x4, local copies, waits for them, and re-layouts  2.67 us

profile of v5, /device:TPU:0, one launch (start us, length us, event | category | flops | bytes accessed | tf_op | source)
XLA Modules:
  0.0 87.3 jit_solution(17845551950171346541)
XLA Ops:
  0.6 84.0 %parareal.1 = (f32[1,3,136,384]{3,2,1,0:T(8,128)}, f32[136,384]{1,0:T(8,128)}) custom-call(s32[136,384]{1,0:T(8,128)} %cls_hbm.1, s32[136,384]{1,0:T(8,128)} %ocean_hbm.1, f32[32]{0:T(128)} %lev_hbm.1, f32[136,384]{1,0:T(8,128)} %drag_hbm.1, f32[2,136,384]{2,1,0:T(8,128)} %force_hbm.1, f32[4,136,384]{2,1,0:T(8,128)} %flow_hbm.1, ...), custom_call_target="tpu_custom_call" | custom-call | tf_op jit(solution)/shard_map/parareal/pallas_call | solution.py:467
  84.6 0.0 copy-start
  84.6 2.0 %copy.12 = f32[1,3,136,384]{3,2,1,0:T(8,128)} copy(f32[1,3,136,384]{3,2,1,0:T(8,128)} %get-tuple-element.4) | data formatting | bytes 1253376
  86.6 0.0 copy-done
  86.6 0.7 copy.13
Async XLA Ops:
  84.6 2.0 %copy-start = (f32[136,384]{1,0:T(8,128)S(1)}, f32[136,384]{1,0:T(8,128)}, u32[]{:S(2)}) copy-start(f32[136,384]{1,0:T(8,128)} %get-tuple-element.5) | copy-start | bytes 626692

commit v6 on v5

--- a/solution.py
+++ b/solution.py
@@ -192,32 +192,35 @@
     def advance(ref, base, offset, start, stop, first, end, want, t):
         cosine = trig_ref[2 * (k * STEPS + t)]
         sine = trig_ref[2 * (k * STEPS + t) + 1]
-        carry = None
-        for r in reversed(range(start, stop, block)):
-            tall = min(block, stop - r)
-            here, there = pl.ds(r, tall), pl.ds(offset + r, tall)
-            a = ref[base, here, :]
+        line = lax.broadcasted_iota(jnp.int32, (TILE, wid), 0)
+        a = ref[base, stop - TILE : stop, :]
+        a_turned = pltpu.roll(a, 1, 0)
+        v_above = None
+        for r in reversed(range(start, stop, TILE)):
+            tall = TILE
+            here, there = pl.ds(r, TILE), pl.ds(offset + r, TILE)
+            if r >= TILE:
+                a_next = ref[base, r - TILE : r, :]
+                next_turned = pltpu.roll(a_next, 1, 0)
+                a_south = jnp.where(line == 0, next_turned, a_turned)
+            else:
+                a_next, next_turned, a_south = a, a_turned, a_turned
             p = st_ref[0, there, :] * ref[base + 1, here, :] - st_ref[2, there, :] * (
                 a - pltpu.roll(a, 1, 1)
             )
-            q = st_ref[1, there, :] * ref[base + 2, here, :] - st_ref[3, there, :] * (
-                a - below(ref, base, r, tall)
-            )
+            q = st_ref[1, there, :] * ref[base + 2, here, :] - st_ref[3, there, :] * (a - a_south)
             u = st_ref[4, there, :] * p
             v = st_ref[5, there, :] * q
-            if carry is None:
-                v_north = pltpu.roll(v, tall - 1, 0)
-            else:
-                v_north = pltpu.roll(
-                    jnp.concatenate([v, carry], axis=0), tall + TILE - 1, 0
-                )[:tall]
-            carry = v[:TILE]
+            v_turned = pltpu.roll(v, TILE - 1, 0)
+            v_north = v_turned if v_above is None else jnp.where(line == TILE - 1, v_above, v_turned)
+            v_above = v_turned
             spread = (pltpu.roll(u, wid - 1, 1) - u) + (v_north - v)
             ref[base, here, :] = st_ref[6, there, :] * (a - spread) + (
                 st_ref[7, there, :] * cosine + st_ref[8, there, :] * sine
             )
             ref[base + 1, here, :] = p
             ref[base + 2, here, :] = q
+            a, a_turned = a_next, next_turned
             low, top = max(r, first), min(r + tall, end)
             if want and low < top:
                 part = pl.ds(offset + low, top - low)

time: 87.5 us -> 87.3 us (level)
  no operation moved by 1% of the time
where the time goes in v6:
time: 87.3 us; the launch traced here: 87.1 us
  Pallas kernels  83.8 us (96%)
  local copies, waits for them, and re-layouts  2.67 us (3%)
    pallas_call x1, Pallas kernels, shards(): pl.pallas_call(functools.partial(kernel, sizes), out_shape=(jax.ShapeDtyp...  83.8 us
    unnamed x4, local copies, waits for them, and re-layouts  2.67 us

profile of v6, /device:TPU:0, one launch (start us, length us, event | category | flops | bytes accessed | tf_op | source)
XLA Modules:
  0.0 87.1 jit_solution(17296114049997047435)
XLA Ops:
  0.6 83.8 %parareal.1 = (f32[1,3,136,384]{3,2,1,0:T(8,128)}, f32[136,384]{1,0:T(8,128)}) custom-call(s32[136,384]{1,0:T(8,128)} %cls_hbm.1, s32[136,384]{1,0:T(8,128)} %ocean_hbm.1, f32[32]{0:T(128)} %lev_hbm.1, f32[136,384]{1,0:T(8,128)} %drag_hbm.1, f32[2,136,384]{2,1,0:T(8,128)} %force_hbm.1, f32[4,136,384]{2,1,0:T(8,128)} %flow_hbm.1, ...), custom_call_target="tpu_custom_call" | custom-call | tf_op jit(solution)/shard_map/parareal/pallas_call | solution.py:470
  84.5 0.0 copy-start
  84.5 2.0 %copy.12 = f32[1,3,136,384]{3,2,1,0:T(8,128)} copy(f32[1,3,136,384]{3,2,1,0:T(8,128)} %get-tuple-element.4) | data formatting | bytes 1253376
  86.5 0.0 copy-done
  86.5 0.7 copy.13
Async XLA Ops:
  84.5 2.0 %copy-start = (f32[136,384]{1,0:T(8,128)S(1)}, f32[136,384]{1,0:T(8,128)}, u32[]{:S(2)}) copy-start(f32[136,384]{1,0:T(8,128)} %get-tuple-element.5) | copy-start | bytes 626692

commit v7 on v5

--- a/solution.py
+++ b/solution.py
@@ -16,7 +16,7 @@
 LANES = 128
 TILE = 8
 EARLY = 8
-SKEW = 5
+SKEW = 4
 
 MESH = pl.DeviceIdType.MESH
 

time: 87.5 us -> 87.6 us (level)
  no operation moved by 1% of the time
where the time goes in v7:
time: 87.6 us; the launch traced here: 87.5 us
  Pallas kernels  84.2 us (96%)
  local copies, waits for them, and re-layouts  2.67 us (3%)
    pallas_call x1, Pallas kernels, shards(): pl.pallas_call(functools.partial(kernel, sizes), out_shape=(jax.ShapeDtyp...  84.2 us
    unnamed x4, local copies, waits for them, and re-layouts  2.67 us

profile of v7, /device:TPU:0, one launch (start us, length us, event | category | flops | bytes accessed | tf_op | source)
XLA Modules:
  0.0 87.5 jit_solution(14269016677656521651)
XLA Ops:
  0.6 84.2 %parareal.1 = (f32[1,3,136,384]{3,2,1,0:T(8,128)}, f32[136,384]{1,0:T(8,128)}) custom-call(s32[136,384]{1,0:T(8,128)} %cls_hbm.1, s32[136,384]{1,0:T(8,128)} %ocean_hbm.1, f32[32]{0:T(128)} %lev_hbm.1, f32[136,384]{1,0:T(8,128)} %drag_hbm.1, f32[2,136,384]{2,1,0:T(8,128)} %force_hbm.1, f32[4,136,384]{2,1,0:T(8,128)} %flow_hbm.1, ...), custom_call_target="tpu_custom_call" | custom-call | tf_op jit(solution)/shard_map/parareal/pallas_call | solution.py:467
  84.8 0.0 copy-start
  84.8 2.0 %copy.12 = f32[1,3,136,384]{3,2,1,0:T(8,128)} copy(f32[1,3,136,384]{3,2,1,0:T(8,128)} %get-tuple-element.4) | data formatting | bytes 1253376
  86.8 0.0 copy-done
  86.8 0.7 copy.13
Async XLA Ops:
  84.8 2.0 %copy-start = (f32[136,384]{1,0:T(8,128)S(1)}, f32[136,384]{1,0:T(8,128)}, u32[]{:S(2)}) copy-start(f32[136,384]{1,0:T(8,128)} %get-tuple-element.5) | copy-start | bytes 626692
